TPU v7x, 256 devices: a whole 4x4x8 slice. The times are simulated.
256 devices in a mesh: dp: 32 (over y, x, core), section: 8 (over z).
Axes of the slice: x: 4, y: 4, z: 8, core: 2. Of those that a mesh axis runs over, the one named last changes fastest.
Arguments:
- prompts: bfloat16 [9216, 5120], P('dp'), may hold values from -6 to 6
- dest_replica: int32 [32, 32], P('dp'), may hold values from 0 to 31, as said below
- anchor_start: int32 [32, 32], P('dp'), may hold values from 0 to 279, as said below
- pack_anchor: int32 [32, 32], P('dp'), may hold values from 0 to 31, as said below
- prompt_lengths: int32 [32, 32], P('dp'), may hold values from 7 to 9, as said below
- item_pos: int32 [32, 32, 6], P('dp'), may hold values from 0 to 8, as said below
- logged_order: int32 [32, 32, 6], P('dp'), may hold values from 0 to 5, each once within a row
- norm_gain: float32 [8, 5120], P('section'), may hold values from 0.1 to 1.9
- query_map: bfloat16 [8, 128, 128], P('section'), may hold values from -0.5 to 0.5
- key_map: bfloat16 [8, 5120, 512], P('section'), may hold values from -0.078125 to 0.078125
- value_map: bfloat16 [8, 5120, 512], P('section'), may hold values from -0.078125 to 0.078125
- final_gain: float32 [5120], replicated, may hold values from 0.1 to 1.9
- score_vector: bfloat16 [5120], replicated, may hold values from -0.078125 to 0.078125
Outputs:
- slate_loglik: float32 [1024], P(('dp', 'section'))
Inputs may be any that keep to these rules, and one draw needn't show every extreme that they name: `dest_replica`: each row lists every replica once: the destinations of the replica's held prompts in row order. `anchor_start`: a replica's held prompts lie back to back from row 0 in the order of their index, each as long as prompt_lengths gives it at its destination. `pack_anchor`: each row lists every replica once. `prompt_lengths`: the 8 prompts of each micro-batch hold exactly 64 tokens together. `item_pos`: distinct and increasing, below the prompt's length; the last is the prompt's final token. `logged_order`: each row is a permutation of 0 to 5.
All inputs are finite; a program needn't handle non-finite values.
Results may differ from a plain program's by a relative error of at most 0.0085.
Values may be sent and summed in bfloat16 or wider, within the bound.
A program may use at most 128 MiB of HBM per device.

v0:
```python
import jax
import jax.numpy as jnp
from jax import lax
from jax.sharding import PartitionSpec as P

LMAX = 9
LMIN = 7
ITEMS = 6
MICRO = 4


epsilon = 1e-06


def passed_along(value, axis, steps):
    count = lax.axis_size(axis)
    initial, last = (max(0, -steps), min(count, count - steps))
    return lax.ppermute(value, axis, [(source, source + steps) for source in range(initial, last)])


def rms_scale(vectors, scale_gain):
    return (
        vectors
        * lax.rsqrt(jnp.mean(vectors * vectors, axis=-1, keepdims=True) + epsilon)
        * scale_gain
    )


def attend_block(tokens, allowed, scale_gain, query_weight, key_weight, value_weight, groups):
    row_count, feature_count = tokens.shape
    head_width = query_weight.shape[0]
    kv_count = key_weight.shape[1] // head_width
    head_count = feature_count // head_width
    group_size = head_count // kv_count
    block_rows = row_count // groups
    widths = tokens.astype(jnp.float32)
    normed = rms_scale(widths, scale_gain).astype(jnp.bfloat16)
    heads_in = normed.reshape(row_count, head_count, head_width)
    queries = jnp.einsum("rhd,de->rhe", heads_in, query_weight, preferred_element_type=jnp.float32)
    queries = (
        rms_scale(queries, 1.0)
        .astype(jnp.bfloat16)
        .reshape(groups, block_rows, kv_count, group_size, head_width)
    )
    key_heads = jnp.dot(normed, key_weight, preferred_element_type=jnp.float32).reshape(
        row_count, kv_count, head_width
    )
    key_heads = (
        rms_scale(key_heads, 1.0)
        .astype(jnp.bfloat16)
        .reshape(groups, block_rows, kv_count, head_width)
    )
    value_heads = jnp.dot(normed, value_weight, preferred_element_type=jnp.float32).astype(
        jnp.bfloat16
    )
    value_heads = value_heads.reshape(groups, block_rows, kv_count, head_width)
    scores = jnp.einsum(
        "grkje,gske->gkjrs", queries, key_heads, preferred_element_type=jnp.float32
    ) * head_width ** (-0.5)
    raw_weights = jnp.where(allowed[:, None, None], jnp.exp(scores), 0.0)
    weights = (raw_weights / jnp.sum(raw_weights, axis=-1, keepdims=True)).astype(jnp.bfloat16)
    mixture = jnp.einsum(
        "gkjrs,gskd->grkjd", weights, value_heads, preferred_element_type=jnp.float32
    )
    return (widths + mixture.reshape(row_count, feature_count)).astype(jnp.bfloat16)


def slate_terms(hidden, item_rows, ranking, final_gain, score_vector):
    picked = jnp.take(hidden, item_rows.reshape(-1), axis=0).astype(jnp.float32)
    normed = rms_scale(picked, final_gain).astype(jnp.bfloat16)
    scores = jnp.dot(normed, score_vector, preferred_element_type=jnp.float32).reshape(
        ranking.shape
    )
    ordered = jnp.take_along_axis(scores, ranking, axis=1)
    tail_sums = jnp.log(jnp.cumsum(jnp.exp(ordered)[:, ::-1], axis=1)[:, ::-1])
    return jnp.sum(ordered - tail_sums, axis=1)


def body(
    prompts,
    dest_replica,
    anchor_start,
    pack_anchor,
    prompt_lengths,
    item_pos,
    logged_order,
    norm_gain,
    query_map,
    key_map,
    value_map,
    final_gain,
    score_vector,
):
    replicas = lax.axis_size("dp")
    sections = lax.axis_size("section")
    section_now = lax.axis_index("section")
    feature_count = prompts.shape[1]
    slot_rows = prompts.shape[0] // replicas
    per_batch = replicas // MICRO
    batch_rows = per_batch * (LMIN + LMAX) // 2
    replica_ids = jnp.arange(replicas, dtype=jnp.int32)
    matches = dest_replica[0][None, :] == replica_ids[:, None]
    starts = jnp.sum(jnp.where(matches, anchor_start[0][None, :], 0), axis=1)
    source_rows = (starts[:, None] + jnp.arange(slot_rows, dtype=jnp.int32)[None, :]).reshape(-1)
    outgoing = jnp.take(prompts, source_rows, axis=0, mode="clip").reshape(
        replicas, slot_rows, feature_count
    )
    received = lax.all_to_all(outgoing, "dp", split_axis=0, concat_axis=0, tiled=True)
    lengths_mb = prompt_lengths[0].reshape(MICRO, per_batch)
    senders = pack_anchor[0].reshape(MICRO, per_batch)
    item_ids = item_pos[0].reshape(MICRO, per_batch, ITEMS)
    ranking = logged_order[0].reshape(MICRO, per_batch, ITEMS)
    groups = 1
    positions = jnp.arange(batch_rows, dtype=jnp.int32)
    offsets = jnp.cumsum(lengths_mb, axis=1) - lengths_mb
    segment = (
        jnp.sum((offsets[:, None, :] <= positions[None, :, None]).astype(jnp.int32), axis=2) - 1
    )
    within = positions[None, :] - jnp.take_along_axis(offsets, segment, axis=1)
    source = jnp.take_along_axis(senders, segment, axis=1) * slot_rows + within
    flat_received = received.reshape(replicas * slot_rows, feature_count)
    stacked = jnp.take(flat_received, source.reshape(-1), axis=0).reshape(
        MICRO, batch_rows, feature_count
    )
    same_prompt = segment[:, :, None] == segment[:, None, :]
    causal = positions[None, :] <= positions[:, None]
    allowed = (same_prompt & causal[None])[:, None]
    item_rows = offsets[:, :, None] + item_ids

    def advance(step_index, incoming, results):
        batch_now = step_index - section_now
        active = (batch_now >= 0) & (batch_now < MICRO)
        chosen = jnp.clip(batch_now, 0, MICRO - 1)
        first_in = lax.dynamic_index_in_dim(
            stacked, jnp.minimum(step_index, MICRO - 1), 0, keepdims=False
        )
        current = jnp.where(section_now == 0, first_in, incoming)
        mask_now = lax.dynamic_index_in_dim(allowed, chosen, 0, keepdims=False)

        def apply_layer(hidden):
            return attend_block(
                hidden, mask_now, norm_gain[0], query_map[0], key_map[0], value_map[0], groups
            )

        def keep_hidden(hidden):
            return hidden

        output = lax.cond(active, apply_layer, keep_hidden, current)
        rows_now = lax.dynamic_index_in_dim(item_rows, chosen, 0, keepdims=False)
        ranking_now = lax.dynamic_index_in_dim(ranking, chosen, 0, keepdims=False)
        slate_values = slate_terms(output, rows_now, ranking_now, final_gain, score_vector)
        record = active & (section_now == sections - 1) & (jnp.arange(MICRO) == chosen)[:, None]
        results = jnp.where(record, slate_values[None, :], results)
        return (output, results)

    results = jnp.zeros((MICRO, per_batch), jnp.float32)
    output, results = advance(0, jnp.zeros_like(stacked[0]), results)

    def loop_body(step_index, carry):
        previous, results_in = carry
        incoming = passed_along(previous, "section", 1)
        return advance(step_index, incoming, results_in)

    output, results = lax.fori_loop(1, MICRO + sections - 1, loop_body, (output, results))
    return lax.psum_scatter(results.reshape(replicas), "section", scatter_dimension=0, tiled=True)


def solution(mesh):
    return jax.shard_map(
        body,
        mesh=mesh,
        in_specs=(
            P("dp", None),
            P("dp", None),
            P("dp", None),
            P("dp", None),
            P("dp", None),
            P("dp", None, None),
            P("dp", None, None),
            P("section", None),
            P("section", None, None),
            P("section", None, None),
            P("section", None, None),
            P(),
            P(),
        ),
        out_specs=P(("dp", "section")),
        check_vma=False,
    )
```

profile of v0, /device:TPU:6, one launch (start us, length us, event | category | flops | bytes accessed | tf_op | source)
XLA Modules:
  0.0 454.3 jit_solution(13050566793670295865)
XLA Ops:
  1.9 4.3 gather_fusion.2
  6.2 5.2 %reshape.332 = bf16[32,9,5120]{2,1,0:T(8,128)(2,1)} reshape(bf16[288,5120]{1,0:T(8,128)(2,1)} %gather_fusion.2) | data formatting | bytes 5898240 | tf_op jit(solution)/shard_map/reshape | solution.py:105
  11.3 7.7 %all-to-all-start = ((bf16[32,9,5120]{2,1,0:T(8,128)(2,1)}), bf16[32,9,5120]{2,1,0:T(8,128)(2,1)}, u32[]{:S(2)}, u32[]{:S(2)}) async-start(bf16[32,9,5120]{2,1,0:T(8,128)(2,1)} %reshape.332), calls=%async_computation | async-start | bytes 10485760 | tf_op jit(solution)/shard_map/all_to_all | solution.py:108
  27.3 7.8 %copy.59 = bf16[1,5120,512]{1,2,0:T(8,128)(2,1)} copy(bf16[1,5120,512]{2,1,0:T(8,128)(2,1)} %param.34) | data formatting | bytes 10485760
  36.6 43.9 %all-to-all-done = bf16[32,9,5120]{2,1,0:T(8,128)(2,1)} async-done(((bf16[32,9,5120]{2,1,0:T(8,128)(2,1)}), bf16[32,9,5120]{2,1,0:T(8,128)(2,1)}, u32[]{:S(2)}, u32[]{:S(2)}) %all-to-all-start) | async-done | bytes 2949152 | tf_op jit(solution)/shard_map/all_to_all | solution.py:108
  91.5 22.7 %conditional.2 = (bf16[64,5120]{1,0:T(8,128)(2,1)S(1)}) conditional(s32[]{:T(128)} %convert_element_type.85, bf16[64,5120]{1,0:T(8,128)(2,1)S(1)} %fusion.63, (bf16[64,5120]{1,0:T(8,128)(2,1)S(1)}, f32[1,5120]{1,0:T(1,128)S(1)}, bf16[1,5120,512]{2,1,0:T(8,128)(2,1)}, s32[4,64]{1,0:T(4,128)S(1)}, bf16[1,5120,512]{2,1,0:T(8,128)(2,1)}, ...), branch_computations={%region_3.5_spmd, %region_4.10_spmd.clone} | conditional | flops 847061312 | bytes 42642444 | solution.py:148
  93.2 7.9 %copy.72 = bf16[1,5120,512]{1,2,0:T(8,128)(2,1)} copy(bf16[1,5120,512]{2,1,0:T(8,128)(2,1)} %get-tuple-element.538) | data formatting | bytes 10485760 | tf_op jit(solution)/shard_map
  101.1 4.3 multiply_reduce_fusion.3
  117.2 271.2 %while.17 = (s32[]{:T(128)}, bf16[64,5120]{1,0:T(8,128)(2,1)S(1)}, f32[4,8]{1,0:T(4,128)S(1)}, s32[]{:T(128)}, pred[]{:T(512)}, /*index=5*/bf16[4,64,5120]{2,1,0...) while((s32[]{:T(128)}, bf16[64,5120]{1,0:T(8,128)(2,1)S(1)}, ...), condition=%wide.region_22.26_spmd.clone, body=%wide.region_12.25_spmd.clone.sunk | while | flops 850095232 | bytes 75474024 | solution.py:164
  118.9 12.8 %collective-permute-done = bf16[64,5120]{1,0:T(8,128)(2,1)S(1)} collective-permute-done((bf16[64,5120]{1,0:T(8,128)(2,1)S(1)}, bf16[64,5120]{1,0:T(8,128)(2,1)S(1)}, u32[]{:S(2)}, u32[]{:S(2)}) %collective-permute-start) | collective-permute-done | bytes 655392 | tf_op jit(solution)/shard_map/while/body/eval_jaxpr/ppermute | solution.py:18
  132.9 11.0 %conditional.5 = (bf16[64,5120]{1,0:T(8,128)(2,1)S(1)}) conditional(s32[]{:T(128)} %convert_element_type.211, bf16[64,5120]{1,0:T(8,128)(2,1)S(1)} %bitcast_select_fusion.2, (bf16[64,5120]{1,0:T(8,128)(2,1)S(1)}, f32[1,5120]{1,0:T(1,128)S(1)}, bf16[1,5120,512]{2,1,0:T(8,128)(2,1)}, s32[4,64]{1,0:T(4,128)S(1)}, s32[]{:T(128)}, ...), branch_computations={%region_13.16_spmd, %region_14.21_spmd} | conditional | flops 847061312 | bytes 68856920 | solution.py:148
  147.0 4.4 collective-permute-start
  151.7 14.0 %collective-permute-done = bf16[64,5120]{1,0:T(8,128)(2,1)S(1)} collective-permute-done((bf16[64,5120]{1,0:T(8,128)(2,1)S(1)}, bf16[64,5120]{1,0:T(8,128)(2,1)S(1)}, u32[]{:S(2)}, u32[]{:S(2)}) %collective-permute-start) | collective-permute-done | bytes 655392 | tf_op jit(solution)/shard_map/while/body/eval_jaxpr/ppermute | solution.py:18
  166.9 11.0 %conditional.5 = (bf16[64,5120]{1,0:T(8,128)(2,1)S(1)}) conditional(s32[]{:T(128)} %convert_element_type.211, bf16[64,5120]{1,0:T(8,128)(2,1)S(1)} %bitcast_select_fusion.2, (bf16[64,5120]{1,0:T(8,128)(2,1)S(1)}, f32[1,5120]{1,0:T(1,128)S(1)}, bf16[1,5120,512]{2,1,0:T(8,128)(2,1)}, s32[4,64]{1,0:T(4,128)S(1)}, s32[]{:T(128)}, ...), branch_computations={%region_13.16_spmd, %region_14.21_spmd} | conditional | flops 847061312 | bytes 68856920 | solution.py:148
  181.0 4.4 collective-permute-start
  185.7 14.4 %collective-permute-done = bf16[64,5120]{1,0:T(8,128)(2,1)S(1)} collective-permute-done((bf16[64,5120]{1,0:T(8,128)(2,1)S(1)}, bf16[64,5120]{1,0:T(8,128)(2,1)S(1)}, u32[]{:S(2)}, u32[]{:S(2)}) %collective-permute-start) | collective-permute-done | bytes 655392 | tf_op jit(solution)/shard_map/while/body/eval_jaxpr/ppermute | solution.py:18
  201.3 11.0 %conditional.5 = (bf16[64,5120]{1,0:T(8,128)(2,1)S(1)}) conditional(s32[]{:T(128)} %convert_element_type.211, bf16[64,5120]{1,0:T(8,128)(2,1)S(1)} %bitcast_select_fusion.2, (bf16[64,5120]{1,0:T(8,128)(2,1)S(1)}, f32[1,5120]{1,0:T(1,128)S(1)}, bf16[1,5120,512]{2,1,0:T(8,128)(2,1)}, s32[4,64]{1,0:T(4,128)S(1)}, s32[]{:T(128)}, ...), branch_computations={%region_13.16_spmd, %region_14.21_spmd} | conditional | flops 847061312 | bytes 68856920 | solution.py:148
  215.4 4.4 collective-permute-start
  220.1 13.6 %collective-permute-done = bf16[64,5120]{1,0:T(8,128)(2,1)S(1)} collective-permute-done((bf16[64,5120]{1,0:T(8,128)(2,1)S(1)}, bf16[64,5120]{1,0:T(8,128)(2,1)S(1)}, u32[]{:S(2)}, u32[]{:S(2)}) %collective-permute-start) | collective-permute-done | bytes 655392 | tf_op jit(solution)/shard_map/while/body/eval_jaxpr/ppermute | solution.py:18
  238.0 15.4 %collective-permute-start = (bf16[64,5120]{1,0:T(8,128)(2,1)S(1)}, bf16[64,5120]{1,0:T(8,128)(2,1)S(1)}, u32[]{:S(2)}, u32[]{:S(2)}) collective-permute-start(bf16[64,5120]{1,0:T(8,128)(2,1)S(1)} %get-tuple-element.730), channel_id=1, source_target_pairs={{0,1},{1,2},{2,3},{3,4},{4,5},{5,6},{6,7},{8,9},{9,10},{10,11},{11... | collective-permute-start | bytes 1966088 | tf_op jit(solution)/shard_map/while/body/eval_jaxpr/ppermute | solution.py:18
  253.8 12.8 %collective-permute-done = bf16[64,5120]{1,0:T(8,128)(2,1)S(1)} collective-permute-done((bf16[64,5120]{1,0:T(8,128)(2,1)S(1)}, bf16[64,5120]{1,0:T(8,128)(2,1)S(1)}, u32[]{:S(2)}, u32[]{:S(2)}) %collective-permute-start) | collective-permute-done | bytes 655392 | tf_op jit(solution)/shard_map/while/body/eval_jaxpr/ppermute | solution.py:18
  270.8 4.4 collective-permute-start
  275.5 11.8 %collective-permute-done = bf16[64,5120]{1,0:T(8,128)(2,1)S(1)} collective-permute-done((bf16[64,5120]{1,0:T(8,128)(2,1)S(1)}, bf16[64,5120]{1,0:T(8,128)(2,1)S(1)}, u32[]{:S(2)}, u32[]{:S(2)}) %collective-permute-start) | collective-permute-done | bytes 655392 | tf_op jit(solution)/shard_map/while/body/eval_jaxpr/ppermute | solution.py:18
  291.6 13.9 %collective-permute-start = (bf16[64,5120]{1,0:T(8,128)(2,1)S(1)}, bf16[64,5120]{1,0:T(8,128)(2,1)S(1)}, u32[]{:S(2)}, u32[]{:S(2)}) collective-permute-start(bf16[64,5120]{1,0:T(8,128)(2,1)S(1)} %get-tuple-element.730), channel_id=1, source_target_pairs={{0,1},{1,2},{2,3},{3,4},{4,5},{5,6},{6,7},{8,9},{9,10},{10,11},{11... | collective-permute-start | bytes 1966088 | tf_op jit(solution)/shard_map/while/body/eval_jaxpr/ppermute | solution.py:18
  305.8 11.1 %collective-permute-done = bf16[64,5120]{1,0:T(8,128)(2,1)S(1)} collective-permute-done((bf16[64,5120]{1,0:T(8,128)(2,1)S(1)}, bf16[64,5120]{1,0:T(8,128)(2,1)S(1)}, u32[]{:S(2)}, u32[]{:S(2)}) %collective-permute-start) | collective-permute-done | bytes 655392 | tf_op jit(solution)/shard_map/while/body/eval_jaxpr/ppermute | solution.py:18
  321.2 4.4 collective-permute-start
  325.9 10.2 %collective-permute-done = bf16[64,5120]{1,0:T(8,128)(2,1)S(1)} collective-permute-done((bf16[64,5120]{1,0:T(8,128)(2,1)S(1)}, bf16[64,5120]{1,0:T(8,128)(2,1)S(1)}, u32[]{:S(2)}, u32[]{:S(2)}) %collective-permute-start) | collective-permute-done | bytes 655392 | tf_op jit(solution)/shard_map/while/body/eval_jaxpr/ppermute | solution.py:18
  340.4 14.6 %collective-permute-start = (bf16[64,5120]{1,0:T(8,128)(2,1)S(1)}, bf16[64,5120]{1,0:T(8,128)(2,1)S(1)}, u32[]{:S(2)}, u32[]{:S(2)}) collective-permute-start(bf16[64,5120]{1,0:T(8,128)(2,1)S(1)} %get-tuple-element.730), channel_id=1, source_target_pairs={{0,1},{1,2},{2,3},{3,4},{4,5},{5,6},{6,7},{8,9},{9,10},{10,11},{11... | collective-permute-start | bytes 1966088 | tf_op jit(solution)/shard_map/while/body/eval_jaxpr/ppermute | solution.py:18
  355.3 9.6 %collective-permute-done = bf16[64,5120]{1,0:T(8,128)(2,1)S(1)} collective-permute-done((bf16[64,5120]{1,0:T(8,128)(2,1)S(1)}, bf16[64,5120]{1,0:T(8,128)(2,1)S(1)}, u32[]{:S(2)}, u32[]{:S(2)}) %collective-permute-start) | collective-permute-done | bytes 655392 | tf_op jit(solution)/shard_map/while/body/eval_jaxpr/ppermute | solution.py:18
  369.2 5.9 %collective-permute-start = (bf16[64,5120]{1,0:T(8,128)(2,1)S(1)}, bf16[64,5120]{1,0:T(8,128)(2,1)S(1)}, u32[]{:S(2)}, u32[]{:S(2)}) collective-permute-start(bf16[64,5120]{1,0:T(8,128)(2,1)S(1)} %get-tuple-element.730), channel_id=1, source_target_pairs={{0,1},{1,2},{2,3},{3,4},{4,5},{5,6},{6,7},{8,9},{9,10},{10,11},{11... | collective-permute-start | bytes 1966088 | tf_op jit(solution)/shard_map/while/body/eval_jaxpr/ppermute | solution.py:18
  375.3 8.8 %collective-permute-done = bf16[64,5120]{1,0:T(8,128)(2,1)S(1)} collective-permute-done((bf16[64,5120]{1,0:T(8,128)(2,1)S(1)}, bf16[64,5120]{1,0:T(8,128)(2,1)S(1)}, u32[]{:S(2)}, u32[]{:S(2)}) %collective-permute-start) | collective-permute-done | bytes 655392 | tf_op jit(solution)/shard_map/while/body/eval_jaxpr/ppermute | solution.py:18
  388.5 65.3 %all-reduce = f32[32]{0:T(128)S(1)} all-reduce(f32[32]{0:T(128)S(1)} %reshape.337), channel_id=2, replica_groups=mesh['dp'=32,'section'=8] {'section'}, use_global_device_ids=true, to_apply=%region_23.27.clone | all-reduce | flops 32 | bytes 256
  (414 shorter events, 114.1 us)
Async XLA Ops:
  0.0 1.9 copy-start
  11.3 8.4 %copy-start.10 = (s32[1,32]{1,0:T(1,128)S(1)}, s32[1,32]{1,0:T(1,128)}, u32[]{:S(2)}) copy-start(s32[1,32]{1,0:T(1,128)} %param.29) | copy-start | bytes 388
  11.3 69.1 %all-to-all-start = ((bf16[32,9,5120]{2,1,0:T(8,128)(2,1)}), bf16[32,9,5120]{2,1,0:T(8,128)(2,1)}, u32[]{:S(2)}, u32[]{:S(2)}) async-start(bf16[32,9,5120]{2,1,0:T(8,128)(2,1)} %reshape.332), calls=%async_computation | async-start | bytes 10485760 | tf_op jit(solution)/shard_map/all_to_all | solution.py:108
  19.1 4.4 copy-start.11
  23.3 3.5 copy-start.7
  23.3 3.8 copy-start.6
  23.4 3.8 copy-start.8
  27.3 7.9 %copy-start.12 = (u32[256]{0:T(256)S(1)}, u32[256]{0:T(256)}, u32[]{:S(2)}) copy-start(u32[256]{0:T(256)} %constant.298) | copy-start | bytes 3076
  89.9 1.5 copy-start.3
  89.9 1.5 copy-start.4
  90.0 1.5 copy-start.5
  114.2 1.2 copy-start.9
  117.2 14.5 %collective-permute-start = (bf16[64,5120]{1,0:T(8,128)(2,1)S(1)}, bf16[64,5120]{1,0:T(8,128)(2,1)S(1)}, u32[]{:S(2)}, u32[]{:S(2)}) collective-permute-start(bf16[64,5120]{1,0:T(8,128)(2,1)S(1)} %get-tuple-element.730), channel_id=1, source_target_pairs={{0,1},{1,2},{2,3},{3,4},{4,5},{5,6},{6,7},{8,9},{9,10},{10,11},{11... | collective-permute-start | bytes 1966088 | tf_op jit(solution)/shard_map/while/body/eval_jaxpr/ppermute | solution.py:18
  133.5 2.5 copy-start.2
  134.5 4.2 slice-start
  136.0 2.8 slice-start.1
  147.0 18.7 %collective-permute-start = (bf16[64,5120]{1,0:T(8,128)(2,1)S(1)}, bf16[64,5120]{1,0:T(8,128)(2,1)S(1)}, u32[]{:S(2)}, u32[]{:S(2)}) collective-permute-start(bf16[64,5120]{1,0:T(8,128)(2,1)S(1)} %get-tuple-element.730), channel_id=1, source_target_pairs={{0,1},{1,2},{2,3},{3,4},{4,5},{5,6},{6,7},{8,9},{9,10},{10,11},{11... | collective-permute-start | bytes 1966088 | tf_op jit(solution)/shard_map/while/body/eval_jaxpr/ppermute | solution.py:18
  167.5 2.5 copy-start.2
  168.5 4.2 slice-start
  170.0 2.8 slice-start.1
  181.0 19.1 %collective-permute-start = (bf16[64,5120]{1,0:T(8,128)(2,1)S(1)}, bf16[64,5120]{1,0:T(8,128)(2,1)S(1)}, u32[]{:S(2)}, u32[]{:S(2)}) collective-permute-start(bf16[64,5120]{1,0:T(8,128)(2,1)S(1)} %get-tuple-element.730), channel_id=1, source_target_pairs={{0,1},{1,2},{2,3},{3,4},{4,5},{5,6},{6,7},{8,9},{9,10},{10,11},{11... | collective-permute-start | bytes 1966088 | tf_op jit(solution)/shard_map/while/body/eval_jaxpr/ppermute | solution.py:18
  201.9 2.5 copy-start.2
  202.9 4.2 slice-start
  204.4 2.8 slice-start.1
  215.4 18.3 %collective-permute-start = (bf16[64,5120]{1,0:T(8,128)(2,1)S(1)}, bf16[64,5120]{1,0:T(8,128)(2,1)S(1)}, u32[]{:S(2)}, u32[]{:S(2)}) collective-permute-start(bf16[64,5120]{1,0:T(8,128)(2,1)S(1)} %get-tuple-element.730), channel_id=1, source_target_pairs={{0,1},{1,2},{2,3},{3,4},{4,5},{5,6},{6,7},{8,9},{9,10},{10,11},{11... | collective-permute-start | bytes 1966088 | tf_op jit(solution)/shard_map/while/body/eval_jaxpr/ppermute | solution.py:18
  238.0 28.5 %collective-permute-start = (bf16[64,5120]{1,0:T(8,128)(2,1)S(1)}, bf16[64,5120]{1,0:T(8,128)(2,1)S(1)}, u32[]{:S(2)}, u32[]{:S(2)}) collective-permute-start(bf16[64,5120]{1,0:T(8,128)(2,1)S(1)} %get-tuple-element.730), channel_id=1, source_target_pairs={{0,1},{1,2},{2,3},{3,4},{4,5},{5,6},{6,7},{8,9},{9,10},{10,11},{11... | collective-permute-start | bytes 1966088 | tf_op jit(solution)/shard_map/while/body/eval_jaxpr/ppermute | solution.py:18
  270.8 16.5 %collective-permute-start = (bf16[64,5120]{1,0:T(8,128)(2,1)S(1)}, bf16[64,5120]{1,0:T(8,128)(2,1)S(1)}, u32[]{:S(2)}, u32[]{:S(2)}) collective-permute-start(bf16[64,5120]{1,0:T(8,128)(2,1)S(1)} %get-tuple-element.730), channel_id=1, source_target_pairs={{0,1},{1,2},{2,3},{3,4},{4,5},{5,6},{6,7},{8,9},{9,10},{10,11},{11... | collective-permute-start | bytes 1966088 | tf_op jit(solution)/shard_map/while/body/eval_jaxpr/ppermute | solution.py:18
  291.6 25.3 %collective-permute-start = (bf16[64,5120]{1,0:T(8,128)(2,1)S(1)}, bf16[64,5120]{1,0:T(8,128)(2,1)S(1)}, u32[]{:S(2)}, u32[]{:S(2)}) collective-permute-start(bf16[64,5120]{1,0:T(8,128)(2,1)S(1)} %get-tuple-element.730), channel_id=1, source_target_pairs={{0,1},{1,2},{2,3},{3,4},{4,5},{5,6},{6,7},{8,9},{9,10},{10,11},{11... | collective-permute-start | bytes 1966088 | tf_op jit(solution)/shard_map/while/body/eval_jaxpr/ppermute | solution.py:18
  321.2 14.9 %collective-permute-start = (bf16[64,5120]{1,0:T(8,128)(2,1)S(1)}, bf16[64,5120]{1,0:T(8,128)(2,1)S(1)}, u32[]{:S(2)}, u32[]{:S(2)}) collective-permute-start(bf16[64,5120]{1,0:T(8,128)(2,1)S(1)} %get-tuple-element.730), channel_id=1, source_target_pairs={{0,1},{1,2},{2,3},{3,4},{4,5},{5,6},{6,7},{8,9},{9,10},{10,11},{11... | collective-permute-start | bytes 1966088 | tf_op jit(solution)/shard_map/while/body/eval_jaxpr/ppermute | solution.py:18
  340.4 24.5 %collective-permute-start = (bf16[64,5120]{1,0:T(8,128)(2,1)S(1)}, bf16[64,5120]{1,0:T(8,128)(2,1)S(1)}, u32[]{:S(2)}, u32[]{:S(2)}) collective-permute-start(bf16[64,5120]{1,0:T(8,128)(2,1)S(1)} %get-tuple-element.730), channel_id=1, source_target_pairs={{0,1},{1,2},{2,3},{3,4},{4,5},{5,6},{6,7},{8,9},{9,10},{10,11},{11... | collective-permute-start | bytes 1966088 | tf_op jit(solution)/shard_map/while/body/eval_jaxpr/ppermute | solution.py:18
  369.2 15.0 %collective-permute-start = (bf16[64,5120]{1,0:T(8,128)(2,1)S(1)}, bf16[64,5120]{1,0:T(8,128)(2,1)S(1)}, u32[]{:S(2)}, u32[]{:S(2)}) collective-permute-start(bf16[64,5120]{1,0:T(8,128)(2,1)S(1)} %get-tuple-element.730), channel_id=1, source_target_pairs={{0,1},{1,2},{2,3},{3,4},{4,5},{5,6},{6,7},{8,9},{9,10},{10,11},{11... | collective-permute-start | bytes 1966088 | tf_op jit(solution)/shard_map/while/body/eval_jaxpr/ppermute | solution.py:18
  388.4 65.9 %copy-start.1 = (bf16[288,5120]{1,0:T(8,128)(2,1)S(1)}, bf16[288,5120]{1,0:T(8,128)(2,1)}, u32[]{:S(2)}) copy-start(bf16[288,5120]{1,0:T(8,128)(2,1)} %param.25) | copy-start | bytes 8847364
where the time goes:
time: 456 us; the launch traced here: 454 us
  waiting for transfers between devices  163 us (36%)
  starting transfers between devices  81 us (18%)
  local copies, waits for them, and re-layouts  80.3 us (18%)
  blocking collectives  65.3 us (14%)
  other arithmetic  34.6 us (8%)
  matrix products  27.3 us (6%)
    ppermute x10, waiting for transfers between devices, passed_along(): lax.ppermute(value, axis, [(source, source + steps) for source in range(i...  119 us
    ppermute x10, starting transfers between devices, passed_along(): lax.ppermute(value, axis, [(source, source + steps) for source in range(i...  73.3 us
    unnamed x1, blocking collectives  65.3 us
    all_to_all x1, waiting for transfers between devices, body(): lax.all_to_all(outgoing, 'dp', split_axis=0, concat_axis=0, tiled=True)  43.9 us
    unnamed x31, local copies, waits for them, and re-layouts  12.1 us
    select_n x11, other arithmetic, advance(): current = jnp.where(section_now == 0, first_in, incoming)  11.8 us
    gather x33, local copies, waits for them, and re-layouts, slate_terms(): ordered = jnp.take_along_axis(scores, ranking, axis=1)  11.4 us
    dot_general x4, matrix products, attend_block(): jnp.dot(normed, key_weight, preferred_element_type=jnp.float32)  9.78 us
  transfers between devices with their start and end apart: 11, of which 11 were waited for; matrix products, arithmetic and copies ran while one was open for 4% of the time, Pallas kernels for 0%

commit v1 on v0

v1 whole, which is shorter than its diff:
```python
import functools

import jax
import jax.numpy as jnp
from jax import lax
from jax.experimental import pallas as pl
from jax.experimental.pallas import tpu as pltpu
from jax.sharding import PartitionSpec as P

EPS = 1e-06
HEAD = 128
GROUPS = 4
ITEMS = 6
LMAX = 9
CHUNK = 16
TAIL = 16
WINDOW = CHUNK + TAIL
PIECES = 4

BF16 = jnp.bfloat16
F32 = jnp.float32
MESH = pl.DeviceIdType.MESH


def iota(shape, dim):
    return lax.broadcasted_iota(jnp.int32, shape, dim)


def kernel(
    sections,
    replicas,
    prompts,
    dest,
    start,
    pack,
    items,
    order,
    gain,
    query,
    key_map,
    value_map,
    final_gain,
    score_vector,
    out,
    x,
    kw,
    vw,
    kv,
    pair,
    kblock,
    vblock,
    bias,
    ones_q,
    ones_k,
    weigh,
    start_row,
    target,
    windows,
    gathered,
    final,
    x_sem,
    w_sem,
    recv_sem,
    send_sem,
    score_send,
    score_recv,
    out_send,
    out_recv,
):
    d = lax.axis_index("dp")
    s = lax.axis_index("section")
    rows_all, width = x.shape
    chunks = rows_all // CHUNK
    last = sections - 1
    heads = width // HEAD
    per_group = heads // GROUPS
    kv_width = GROUPS * HEAD
    above = lax.rem(s + 1, sections)
    below = lax.rem(s + sections - 1, sections)

    def chunk_rows(c):
        return pl.ds(pl.multiple_of(c * CHUNK, 16), CHUNK)

    def x_copy(c):
        return pltpu.make_async_copy(prompts.at[chunk_rows(c)], x.at[chunk_rows(c)], x_sem.at[c])

    def hop(c):
        return pltpu.make_async_remote_copy(
            x.at[chunk_rows(c)], x.at[chunk_rows(c)], send_sem.at[c], recv_sem.at[c],
            device_id=(d, above), device_id_type=MESH,
        )

    piece = width // PIECES

    def w_copies():
        copies = []
        for p in range(PIECES):
            part = pl.ds(p * piece, piece)
            copies.append(pltpu.make_async_copy(key_map.at[0, part], kw.at[part], w_sem.at[0, p]))
            copies.append(pltpu.make_async_copy(value_map.at[0, part], vw.at[part], w_sem.at[1, p]))
        return copies

    @pl.when(s == 0)
    def _():
        x_copy(0).start()

    for copy in w_copies():
        copy.start()

    @pl.when(s == 0)
    def _():
        def fetch(c, carry):
            x_copy(c).start()
            return carry

        lax.fori_loop(1, chunks, fetch, 0)

    barrier = pltpu.get_barrier_semaphore()
    pl.semaphore_signal(barrier, inc=1, device_id=(d, above), device_id_type=MESH)
    pl.semaphore_signal(barrier, inc=1, device_id=(d, below), device_id_type=MESH)

    @pl.when(s < last)
    def _():
        pl.semaphore_signal(barrier, inc=1, device_id=(d, last), device_id_type=MESH)

    @pl.when(s == last)
    def _():
        def greet_section(i, carry):
            pl.semaphore_signal(barrier, inc=1, device_id=(d, i), device_id_type=MESH)
            return carry

        def greet_replica(i, carry):
            peer = lax.rem(d + i, replicas)
            pl.semaphore_signal(barrier, inc=1, device_id=(peer, last), device_id_type=MESH)
            return carry

        lax.fori_loop(0, last, greet_section, 0)
        lax.fori_loop(1, replicas, greet_replica, 0)

    pair[...] = jnp.zeros_like(pair)
    pair[0:HEAD, 0:HEAD] = query[0]
    pair[HEAD : 2 * HEAD, HEAD : 2 * HEAD] = query[0]
    kblock[...] = jnp.zeros_like(kblock)
    vblock[...] = jnp.zeros_like(vblock)
    kv[0:TAIL, :] = jnp.zeros((TAIL, 2 * kv_width), BF16)
    ones_q[...] = jnp.where(
        iota(ones_q.shape, 0) // HEAD == iota(ones_q.shape, 1) // WINDOW, 1.0, 0.0
    ).astype(BF16)
    ones_k[...] = jnp.where(
        iota(ones_k.shape, 0) // WINDOW == iota(ones_k.shape, 1) // WINDOW, 1.0, 0.0
    ).astype(BF16)

    starts = start[...].astype(F32)
    for c in range(chunks):
        row = (iota((CHUNK, replicas), 0) + c * CHUNK).astype(F32)
        first = jnp.max(jnp.where(starts <= row, starts, 0.0), axis=1, keepdims=True)
        seen = (iota((CHUNK, GROUPS * WINDOW), 1) % WINDOW + c * CHUNK - TAIL).astype(F32)
        own = (iota((CHUNK, GROUPS * WINDOW), 0) + c * CHUNK).astype(F32)
        bias[c] = jnp.where((seen >= first) & (seen <= own), 0.0, -1e30)

    square = (replicas, replicas)

    @pl.when(s == last)
    def _():
        weigh[...] = final_gain[...] * score_vector[...].astype(F32).reshape(1, width)
        column = jnp.sum(
            jnp.where(dest[...] == iota(square, 0), starts, 0.0), axis=1, keepdims=True
        )
        start_row[0:1, 0:replicas] = jnp.sum(
            jnp.where(iota(square, 0) == iota(square, 1), column, 0.0), axis=0, keepdims=True
        )
        origin = pack[...].astype(F32) * 16.0
        for k in range(ITEMS):
            place = origin
            for i in range(ITEMS):
                place = place + jnp.where(order[k] == i, items[i].astype(F32), 0.0)
            target[k : k + 1, 0:replicas] = place
        windows[...] = jnp.zeros_like(windows)

    @pl.when(s < last)
    def _():
        pl.semaphore_wait(barrier, 3)

    @pl.when(s == last)
    def _():
        pl.semaphore_wait(barrier, last + replicas + 1)

    for copy in w_copies():
        copy.wait()

    def scale_of(states):
        return lax.rsqrt(jnp.mean(states * states, axis=1, keepdims=True) + EPS)

    def by_group(values):
        def head(a):
            p, half = divmod(a, 2)
            return values[p * CHUNK : (p + 1) * CHUNK, half * HEAD : (half + 1) * HEAD]

        return jnp.concatenate(
            [
                jnp.concatenate([head(b * per_group + j) for b in range(GROUPS)], axis=1)
                for j in range(per_group)
            ],
            axis=0,
        )

    def block(c):
        states = x[chunk_rows(c), :].astype(F32)
        normed = (states * scale_of(states) * gain[...]).astype(BF16)
        keys = jnp.dot(normed, kw[...], preferred_element_type=F32)
        parts = []
        for b in range(GROUPS):
            head = keys[:, b * HEAD : (b + 1) * HEAD]
            parts.append((head * scale_of(head)).astype(BF16))
        parts.append(jnp.dot(normed, vw[...], preferred_element_type=F32).astype(BF16))
        fresh = jnp.concatenate(parts, axis=1)
        old = kv[...]
        kv[...] = fresh
        stacked = jnp.concatenate(
            [normed[:, p * 2 * HEAD : (p + 1) * 2 * HEAD] for p in range(heads // 2)], axis=0
        )
        q = jnp.dot(stacked, pair[...], preferred_element_type=F32)
        squares = jnp.dot(by_group((q * q).astype(BF16)), ones_q[...], preferred_element_type=F32)
        for b in range(GROUPS):
            cols = slice(b * HEAD, (b + 1) * HEAD)
            more = slice(kv_width + b * HEAD, kv_width + (b + 1) * HEAD)
            for place, part in ((0, old), (TAIL, fresh)):
                rows = slice(b * WINDOW + place, b * WINDOW + place + 16)
                kblock[rows, cols] = part[:, cols]
                vblock[rows, cols] = part[:, more]
        raw = lax.dot_general(
            by_group(q.astype(BF16)), kblock[...], (((1,), (1,)), ((), ())), preferred_element_type=F32
        )
        scores = raw * (lax.rsqrt(squares * (1.0 / HEAD) + EPS) * HEAD ** (-0.5))
        powers = jnp.exp(scores + jnp.concatenate([bias[c]] * per_group, axis=0))
        total = jnp.dot(powers.astype(BF16), ones_k[...], preferred_element_type=F32)
        weights = (powers / total).astype(BF16)
        mixed = jnp.dot(weights, vblock[...], preferred_element_type=F32)
        placed = [
            mixed[j * CHUNK : (j + 1) * CHUNK, b * HEAD : (b + 1) * HEAD]
            for b in range(GROUPS)
            for j in range(per_group)
        ]
        x[chunk_rows(c), :] = (states + jnp.concatenate(placed, axis=1)).astype(BF16)

    def finish(c):
        states = x[chunk_rows(c), :].astype(F32)
        value = jnp.sum(states * weigh[...], axis=1, keepdims=True) * scale_of(states)
        row = (iota((CHUNK, replicas), 0) + c * CHUNK).astype(F32)
        offset = row - start_row[0:1, 0:replicas]
        found = [
            jnp.sum(jnp.where(offset == float(i), value, 0.0), axis=0, keepdims=True) for i in range(LMAX)
        ]
        found.append(jnp.zeros((16 - LMAX, replicas), F32))
        windows[:, 0:replicas] += jnp.concatenate(found, axis=0)

    def advance(c, carry):
        @pl.when(s == 0)
        def _():
            x_copy(c).wait()

        @pl.when(s > 0)
        def _():
            hop(c).wait_recv()

        block(c)

        @pl.when(s < last)
        def _():
            hop(c).start()

        @pl.when(s == last)
        def _():
            finish(c)

        return carry

    lax.fori_loop(0, chunks, advance, 0)

    @pl.when(s == last)
    def _():
        def score_copy(peer, slot):
            return pltpu.make_async_remote_copy(
                windows, gathered.at[slot], score_send.at[peer], score_recv.at[slot],
                device_id=(peer, last), device_id_type=MESH,
            )

        def send(i, carry):
            score_copy(lax.rem(d + i, replicas), d).start()
            return carry

        def receive(i, carry):
            peer = lax.rem(d + i, replicas)
            score_copy(peer, peer).wait_recv()
            return carry

        def sent(i, carry):
            score_copy(lax.rem(d + i, replicas), d).wait_send()
            return carry

        lax.fori_loop(1, replicas, send, 0)
        gathered[d] = windows[...]
        lax.fori_loop(1, replicas, receive, 0)
        mine = jnp.sum(
            jnp.where(iota(gathered.shape, 2) == d, gathered[...], 0.0), axis=2, keepdims=True
        ).reshape(replicas * 16, 1)
        place = iota((replicas * 16, replicas), 0).astype(F32)
        ordered = [
            jnp.sum(jnp.where(place == target[k : k + 1, 0:replicas], mine, 0.0), axis=0, keepdims=True)
            for k in range(ITEMS)
        ]
        tail = jnp.zeros((1, replicas), F32)
        total = jnp.zeros((1, replicas), F32)
        for k in reversed(range(ITEMS)):
            tail = tail + jnp.exp(ordered[k])
            total = total + (ordered[k] - jnp.log(tail))
        final[0:1, 0:replicas] = total

        def out_copy(i):
            return pltpu.make_async_remote_copy(
                final, final, out_send.at[i], out_recv.at[0], device_id=(d, i), device_id_type=MESH
            )

        def send_out(i, carry):
            out_copy(i).start()
            return carry

        def sent_out(i, carry):
            out_copy(i).wait_send()
            return carry

        lax.fori_loop(0, last, send_out, 0)
        lax.fori_loop(1, replicas, sent, 0)
        lax.fori_loop(0, last, sent_out, 0)

    @pl.when(s < last)
    def _():
        def sent_hop(c, carry):
            hop(c).wait_send()
            return carry

        lax.fori_loop(0, chunks, sent_hop, 0)

    @pl.when(s < last)
    def _():
        pltpu.make_async_remote_copy(
            final, final, out_send.at[0], out_recv.at[0], device_id=(d, last), device_id_type=MESH
        ).wait_recv()

    values = final[0:1, :]
    share = replicas // sections
    for j in range(share):
        out[j] = jnp.sum(jnp.where(iota(values.shape, 1) == s * share + j, values, 0.0))


def body(
    prompts,
    dest_replica,
    anchor_start,
    pack_anchor,
    prompt_lengths,
    item_pos,
    logged_order,
    norm_gain,
    query_map,
    key_map,
    value_map,
    final_gain,
    score_vector,
):
    sections = lax.axis_size("section")
    replicas = lax.axis_size("dp")
    rows, width = prompts.shape
    chunks = rows // CHUNK
    kv_width = GROUPS * HEAD
    whole = pl.BlockSpec(memory_space=pltpu.VMEM)
    held = pl.BlockSpec(memory_space=pl.ANY)
    return pl.pallas_call(
        functools.partial(kernel, sections, replicas),
        out_shape=jax.ShapeDtypeStruct((replicas // sections,), F32),
        in_specs=[held] + [whole] * 7 + [held, held] + [whole] * 2,
        out_specs=pl.BlockSpec(memory_space=pltpu.SMEM),
        scratch_shapes=[
            pltpu.VMEM((rows, width), BF16),
            pltpu.VMEM((width, kv_width), BF16),
            pltpu.VMEM((width, kv_width), BF16),
            pltpu.VMEM((TAIL, 2 * kv_width), BF16),
            pltpu.VMEM((2 * HEAD, 2 * HEAD), BF16),
            pltpu.VMEM((GROUPS * WINDOW, kv_width), BF16),
            pltpu.VMEM((GROUPS * WINDOW, kv_width), BF16),
            pltpu.VMEM((chunks, CHUNK, GROUPS * WINDOW), F32),
            pltpu.VMEM((kv_width, GROUPS * WINDOW), BF16),
            pltpu.VMEM((GROUPS * WINDOW, GROUPS * WINDOW), BF16),
            pltpu.VMEM((1, width), F32),
            pltpu.VMEM((8, 128), F32),
            pltpu.VMEM((8, 128), F32),
            pltpu.VMEM((16, 128), F32),
            pltpu.VMEM((replicas, 16, 128), F32),
            pltpu.VMEM((8, 128), F32),
            pltpu.SemaphoreType.DMA((chunks,)),
            pltpu.SemaphoreType.DMA((2, PIECES)),
            pltpu.SemaphoreType.DMA((chunks,)),
            pltpu.SemaphoreType.DMA((chunks,)),
            pltpu.SemaphoreType.DMA((replicas,)),
            pltpu.SemaphoreType.DMA((replicas,)),
            pltpu.SemaphoreType.DMA((sections,)),
            pltpu.SemaphoreType.DMA((1,)),
        ],
        compiler_params=pltpu.CompilerParams(
            collective_id=0, has_side_effects=True, vmem_limit_bytes=56 << 20
        ),
        name="slates",
    )(
        prompts,
        dest_replica,
        anchor_start,
        pack_anchor,
        jnp.transpose(item_pos, (2, 0, 1)),
        jnp.transpose(logged_order, (2, 0, 1)),
        norm_gain,
        query_map,
        key_map,
        value_map,
        final_gain.reshape(1, width),
        score_vector,
    )


def solution(mesh):
    return jax.shard_map(
        body,
        mesh=mesh,
        in_specs=(
            P("dp", None),
            P("dp", None),
            P("dp", None),
            P("dp", None),
            P("dp", None),
            P("dp", None, None),
            P("dp", None, None),
            P("section", None),
            P("section", None, None),
            P("section", None, None),
            P("section", None, None),
            P(),
            P(),
        ),
        out_specs=P(("dp", "section")),
        check_vma=False,
    )
```

time: 456 us -> 138 us (0.30)
  waiting for transfers between devices: 163 us -> 0 us
  Pallas kernels: 0 us -> 135 us
  starting transfers between devices: 81 us -> 0 us
  local copies, waits for them, and re-layouts: 80.3 us -> 1.19 us
  blocking collectives: 65.3 us -> 0 us
  other arithmetic: 34.6 us -> 0 us
  matrix products: 27.3 us -> 0 us
    pallas_call x0 -> x1, Pallas kernels: none -> 135 us  [body(): pl.pallas_call(functools.partial(kernel, sections, replicas), out_shape=j...]
    ppermute x10 -> x0, waiting for transfers between devices: 119 us -> none  [passed_along(): lax.ppermute(value, axis, [(source, source + steps) for source in range(i...]
    ppermute x10 -> x0, starting transfers between devices: 73.3 us -> none  [passed_along(): lax.ppermute(value, axis, [(source, source + steps) for source in range(i...]
    unnamed x1 -> x0, blocking collectives: 65.3 us -> none
    all_to_all x1 -> x0, waiting for transfers between devices: 43.9 us -> none  [body(): lax.all_to_all(outgoing, 'dp', split_axis=0, concat_axis=0, tiled=True)]
    gather x51 -> x0, local copies, waits for them, and re-layouts: 33.6 us -> none  [the longest x33 11.4 us: slate_terms(): ordered = jnp.take_along_axis(scores, ranking, axis=1)]
    dot_general x31 -> x0, matrix products: 27.3 us -> none  [the longest x4 9.78 us: attend_block(): jnp.dot(normed, key_weight, preferred_element_type=jnp.float32)]
    reshape x30 -> x0, local copies, waits for them, and re-layouts: 16.4 us -> none  [the longest x4 5.44 us: attend_block(): mixture.reshape(row_count, feature_count)]
  transfers between devices with their start and end apart: 11 -> 0, of which waited for: 11 -> 0; matrix products, arithmetic and copies ran while one was open for 4% -> 0% of each run, Pallas kernels for 0% -> 0%
where the time goes in v1:
time: 138 us; the launch traced here: 137 us
  Pallas kernels  135 us (98%)
    pallas_call x1, Pallas kernels, body(): pl.pallas_call(functools.partial(kernel, sections, replicas), out_shape=j...  135 us

profile of v1, /device:TPU:6, one launch (start us, length us, event | category | flops | bytes accessed | tf_op | source)
XLA Modules:
  0.0 136.7 jit_solution(15557228891157399914)
XLA Ops:
  0.0 135.5 %slates.1 = f32[4]{0:T(128)} custom-call(bf16[288,5120]{1,0:T(8,128)(2,1)} %prompts.1, s32[1,32]{1,0:T(1,128)} %dest.1, s32[1,32]{1,0:T(1,128)} %start.1, s32[1,32]{1,0:T(1,128)} %pack.1, s32[6,1,32]{2,1,0:T(1,128)} %bitcast.4, s32[6,1,32]{2,1,0:T(1,128)} %bitcast.5, f32[1,5120]{1,0:T(1,128)} %gain.1, bf16[1,128,128]{2,1,0:T(8,128)(2,1)} %query.1, ...), custom_call_target="tpu_custom_call" | custom-call | tf_op jit(solution)/shard_map/slates/pallas_call | solution.py:378
  135.5 1.2 copy.14

commit v2 on v1

--- a/solution.py
+++ b/solution.py
@@ -16,6 +16,8 @@
 TAIL = 16
 WINDOW = CHUNK + TAIL
 PIECES = 4
+SPILL = 1024.0
+PARTS = 4
 
 BF16 = jnp.bfloat16
 F32 = jnp.float32
@@ -66,6 +68,7 @@
     score_recv,
     out_send,
     out_recv,
+    turn,
 ):
     d = lax.axis_index("dp")
     s = lax.axis_index("section")
@@ -77,6 +80,7 @@
     kv_width = GROUPS * HEAD
     above = lax.rem(s + 1, sections)
     below = lax.rem(s + sections - 1, sections)
+    twin = d + 1 - 2 * lax.rem(d, 2)
 
     def chunk_rows(c):
         return pl.ds(pl.multiple_of(c * CHUNK, 16), CHUNK)
@@ -84,9 +88,13 @@
     def x_copy(c):
         return pltpu.make_async_copy(prompts.at[chunk_rows(c)], x.at[chunk_rows(c)], x_sem.at[c])
 
-    def hop(c):
+    part = width // PARTS
+    part_groups = GROUPS // PARTS
+
+    def hop(c, p):
+        block = x.at[chunk_rows(c), pl.ds(p * part, part)]
         return pltpu.make_async_remote_copy(
-            x.at[chunk_rows(c)], x.at[chunk_rows(c)], send_sem.at[c], recv_sem.at[c],
+            block, block, send_sem.at[c, p], recv_sem.at[c, p],
             device_id=(d, above), device_id_type=MESH,
         )
 
@@ -122,6 +130,10 @@
     @pl.when(s < last)
     def _():
         pl.semaphore_signal(barrier, inc=1, device_id=(d, last), device_id_type=MESH)
+
+    @pl.when(s == 0)
+    def _():
+        pl.semaphore_signal(barrier, inc=1, device_id=(twin, s), device_id_type=MESH)
 
     @pl.when(s == last)
     def _():
@@ -147,7 +159,7 @@
         iota(ones_q.shape, 0) // HEAD == iota(ones_q.shape, 1) // WINDOW, 1.0, 0.0
     ).astype(BF16)
     ones_k[...] = jnp.where(
-        iota(ones_k.shape, 0) // WINDOW == iota(ones_k.shape, 1) // WINDOW, 1.0, 0.0
+        iota(ones_k.shape, 0) // WINDOW == iota(ones_k.shape, 1) // HEAD, 1.0, 0.0
     ).astype(BF16)
 
     starts = start[...].astype(F32)
@@ -169,15 +181,20 @@
         start_row[0:1, 0:replicas] = jnp.sum(
             jnp.where(iota(square, 0) == iota(square, 1), column, 0.0), axis=0, keepdims=True
         )
-        origin = pack[...].astype(F32) * 16.0
+        away = pack[...] - d
+        slot = jnp.where(away < 0, away + replicas, away).astype(F32) * 8.0
         for k in range(ITEMS):
-            place = origin
+            spot = jnp.zeros((1, replicas), F32)
             for i in range(ITEMS):
-                place = place + jnp.where(order[k] == i, items[i].astype(F32), 0.0)
-            target[k : k + 1, 0:replicas] = place
+                spot = spot + jnp.where(order[k] == i, items[i].astype(F32), 0.0)
+            target[k : k + 1, 0:replicas] = jnp.where(spot < 8.0, slot + spot, slot + SPILL)
         windows[...] = jnp.zeros_like(windows)
 
-    @pl.when(s < last)
+    @pl.when(s == 0)
+    def _():
+        pl.semaphore_wait(barrier, 4)
+
+    @pl.when((s > 0) & (s < last))
     def _():
         pl.semaphore_wait(barrier, 3)
 
@@ -191,57 +208,84 @@
     def scale_of(states):
         return lax.rsqrt(jnp.mean(states * states, axis=1, keepdims=True) + EPS)
 
-    def by_group(values):
-        def head(a):
+    def by_group(parts):
+        def head(b, j):
+            a = (b % part_groups) * per_group + j
             p, half = divmod(a, 2)
+            values = parts[b // part_groups]
             return values[p * CHUNK : (p + 1) * CHUNK, half * HEAD : (half + 1) * HEAD]
 
         return jnp.concatenate(
-            [
-                jnp.concatenate([head(b * per_group + j) for b in range(GROUPS)], axis=1)
-                for j in range(per_group)
-            ],
+            [jnp.concatenate([head(b, j) for b in range(GROUPS)], axis=1) for j in range(per_group)],
             axis=0,
         )
 
     def block(c):
-        states = x[chunk_rows(c), :].astype(F32)
-        normed = (states * scale_of(states) * gain[...]).astype(BF16)
-        keys = jnp.dot(normed, kw[...], preferred_element_type=F32)
-        parts = []
-        for b in range(GROUPS):
-            head = keys[:, b * HEAD : (b + 1) * HEAD]
-            parts.append((head * scale_of(head)).astype(BF16))
-        parts.append(jnp.dot(normed, vw[...], preferred_element_type=F32).astype(BF16))
-        fresh = jnp.concatenate(parts, axis=1)
+        rows = chunk_rows(c)
         old = kv[...]
-        kv[...] = fresh
-        stacked = jnp.concatenate(
-            [normed[:, p * 2 * HEAD : (p + 1) * 2 * HEAD] for p in range(heads // 2)], axis=0
-        )
-        q = jnp.dot(stacked, pair[...], preferred_element_type=F32)
-        squares = jnp.dot(by_group((q * q).astype(BF16)), ones_q[...], preferred_element_type=F32)
+        energy = jnp.zeros((CHUNK, 1), F32)
+        keys = jnp.zeros((CHUNK, kv_width), F32)
+        values = jnp.zeros((CHUNK, kv_width), F32)
+        queries, squares = [], []
+        for p in range(PARTS):
+            @pl.when(s > 0)
+            def _():
+                hop(c, p).wait_recv()
+
+            cols = slice(p * part, (p + 1) * part)
+            states = x[rows, cols].astype(F32)
+            energy = energy + jnp.sum(states * states, axis=1, keepdims=True)
+            gained = (states * gain[:, cols]).astype(BF16)
+            keys = keys + jnp.dot(gained, kw[cols, :], preferred_element_type=F32)
+            values = values + jnp.dot(gained, vw[cols, :], preferred_element_type=F32)
+            stacked = jnp.concatenate(
+                [gained[:, i * 2 * HEAD : (i + 1) * 2 * HEAD] for i in range(part // (2 * HEAD))], axis=0
+            )
+            q = jnp.dot(stacked, pair[...], preferred_element_type=F32)
+            queries.append(q.astype(BF16))
+            squares.append((q * q).astype(BF16))
+        scale = lax.rsqrt(energy * (1.0 / width) + EPS)
+        keys = keys * scale
+        values = (values * scale).astype(BF16)
         for b in range(GROUPS):
             cols = slice(b * HEAD, (b + 1) * HEAD)
             more = slice(kv_width + b * HEAD, kv_width + (b + 1) * HEAD)
-            for place, part in ((0, old), (TAIL, fresh)):
-                rows = slice(b * WINDOW + place, b * WINDOW + place + 16)
-                kblock[rows, cols] = part[:, cols]
-                vblock[rows, cols] = part[:, more]
+            head = keys[:, cols]
+            head = (head * scale_of(head)).astype(BF16)
+            kblock[b * WINDOW : b * WINDOW + TAIL, cols] = old[:, cols]
+            kblock[b * WINDOW + TAIL : (b + 1) * WINDOW, cols] = head
+            kv[:, cols] = head
+            vblock[b * WINDOW : b * WINDOW + TAIL, cols] = old[:, more]
+            vblock[b * WINDOW + TAIL : (b + 1) * WINDOW, cols] = values[:, cols]
+            kv[:, more] = values[:, cols]
+        length = jnp.dot(by_group(squares), ones_q[...], preferred_element_type=F32)
+        scales = jnp.concatenate([scale] * per_group, axis=0)
+        factor = scales * lax.rsqrt(length * (scales * scales * (1.0 / HEAD)) + EPS) * HEAD ** (-0.5)
         raw = lax.dot_general(
-            by_group(q.astype(BF16)), kblock[...], (((1,), (1,)), ((), ())), preferred_element_type=F32
+            by_group(queries), kblock[...], (((1,), (1,)), ((), ())), preferred_element_type=F32
         )
-        scores = raw * (lax.rsqrt(squares * (1.0 / HEAD) + EPS) * HEAD ** (-0.5))
-        powers = jnp.exp(scores + jnp.concatenate([bias[c]] * per_group, axis=0))
-        total = jnp.dot(powers.astype(BF16), ones_k[...], preferred_element_type=F32)
-        weights = (powers / total).astype(BF16)
-        mixed = jnp.dot(weights, vblock[...], preferred_element_type=F32)
-        placed = [
-            mixed[j * CHUNK : (j + 1) * CHUNK, b * HEAD : (b + 1) * HEAD]
-            for b in range(GROUPS)
-            for j in range(per_group)
-        ]
-        x[chunk_rows(c), :] = (states + jnp.concatenate(placed, axis=1)).astype(BF16)
+        powers = jnp.exp(raw * factor + jnp.concatenate([bias[c]] * per_group, axis=0)).astype(BF16)
+        for p in range(PARTS):
+            near = slice(p * part_groups * HEAD, (p + 1) * part_groups * HEAD)
+            cols = slice(p * part, (p + 1) * part)
+            mixed = jnp.dot(powers, vblock[:, near], preferred_element_type=F32)
+            total = jnp.dot(powers, ones_k[:, near], preferred_element_type=F32)
+            mixed = mixed / total
+            placed = [
+                mixed[j * CHUNK : (j + 1) * CHUNK, b * HEAD : (b + 1) * HEAD]
+                for b in range(part_groups)
+                for j in range(per_group)
+            ]
+            x[rows, cols] = (x[rows, cols].astype(F32) + jnp.concatenate(placed, axis=1)).astype(BF16)
+
+            if p == 0:
+                @pl.when((s == 0) & (c == 0) & (lax.rem(d, 2) == 1))
+                def _():
+                    pl.semaphore_wait(turn, 1)
+
+            @pl.when(s < last)
+            def _():
+                hop(c, p).start()
 
     def finish(c):
         states = x[chunk_rows(c), :].astype(F32)
@@ -251,23 +295,19 @@
         found = [
             jnp.sum(jnp.where(offset == float(i), value, 0.0), axis=0, keepdims=True) for i in range(LMAX)
         ]
-        found.append(jnp.zeros((16 - LMAX, replicas), F32))
-        windows[:, 0:replicas] += jnp.concatenate(found, axis=0)
+        windows[:, 0:replicas] += jnp.concatenate(found[0:8], axis=0)
+        windows[0:1, replicas : 2 * replicas] += found[8]
 
     def advance(c, carry):
         @pl.when(s == 0)
         def _():
             x_copy(c).wait()
 
-        @pl.when(s > 0)
+        block(c)
+
+        @pl.when((s == 0) & (c == 0) & (lax.rem(d, 2) == 0))
         def _():
-            hop(c).wait_recv()
-
-        block(c)
-
-        @pl.when(s < last)
-        def _():
-            hop(c).start()
+            pl.semaphore_signal(turn, inc=1, device_id=(twin, s), device_id_type=MESH)
 
         @pl.when(s == last)
         def _():
@@ -279,36 +319,29 @@
 
     @pl.when(s == last)
     def _():
-        def score_copy(peer, slot):
+        def score_copy(i):
+            peer = lax.rem(d + replicas - i, replicas)
             return pltpu.make_async_remote_copy(
-                windows, gathered.at[slot], score_send.at[peer], score_recv.at[slot],
+                windows, gathered.at[i], score_send.at[0], score_recv.at[0],
                 device_id=(peer, last), device_id_type=MESH,
             )
 
-        def send(i, carry):
-            score_copy(lax.rem(d + i, replicas), d).start()
-            return carry
-
-        def receive(i, carry):
-            peer = lax.rem(d + i, replicas)
-            score_copy(peer, peer).wait_recv()
-            return carry
-
-        def sent(i, carry):
-            score_copy(lax.rem(d + i, replicas), d).wait_send()
-            return carry
-
-        lax.fori_loop(1, replicas, send, 0)
-        gathered[d] = windows[...]
-        lax.fori_loop(1, replicas, receive, 0)
-        mine = jnp.sum(
-            jnp.where(iota(gathered.shape, 2) == d, gathered[...], 0.0), axis=2, keepdims=True
-        ).reshape(replicas * 16, 1)
-        place = iota((replicas * 16, replicas), 0).astype(F32)
-        ordered = [
-            jnp.sum(jnp.where(place == target[k : k + 1, 0:replicas], mine, 0.0), axis=0, keepdims=True)
-            for k in range(ITEMS)
-        ]
+        others = gathered.at[pl.ds(1, replicas - 1)]
+        for i in range(1, replicas):
+            score_copy(i).start()
+        gathered[0] = windows[...]
+        pltpu.make_async_copy(others, others, score_recv.at[0]).wait()
+        held = gathered[...]
+        lane = iota(gathered.shape, 2)
+        near = jnp.sum(jnp.where(lane == d, held, 0.0), axis=2, keepdims=True).reshape(replicas * 8, 1)
+        far = jnp.sum(jnp.where(lane == d + replicas, held, 0.0), axis=2, keepdims=True)
+        far = far.reshape(replicas * 8, 1)
+        place = iota((replicas * 8, replicas), 0).astype(F32)
+        ordered = []
+        for k in range(ITEMS):
+            wanted = target[k : k + 1, 0:replicas]
+            picked = jnp.where(place == wanted, near, 0.0) + jnp.where(place + SPILL == wanted, far, 0.0)
+            ordered.append(jnp.sum(picked, axis=0, keepdims=True))
         tail = jnp.zeros((1, replicas), F32)
         total = jnp.zeros((1, replicas), F32)
         for k in reversed(range(ITEMS)):
@@ -321,22 +354,17 @@
                 final, final, out_send.at[i], out_recv.at[0], device_id=(d, i), device_id_type=MESH
             )
 
-        def send_out(i, carry):
+        for i in sorted(range(last), key=lambda i: -min(i + 1, last - i)):
             out_copy(i).start()
-            return carry
-
-        def sent_out(i, carry):
+        pltpu.make_async_copy(others, others, score_send.at[0]).wait()
+        for i in range(last):
             out_copy(i).wait_send()
-            return carry
-
-        lax.fori_loop(0, last, send_out, 0)
-        lax.fori_loop(1, replicas, sent, 0)
-        lax.fori_loop(0, last, sent_out, 0)
 
     @pl.when(s < last)
     def _():
         def sent_hop(c, carry):
-            hop(c).wait_send()
+            for p in range(PARTS):
+                hop(c, p).wait_send()
             return carry
 
         lax.fori_loop(0, chunks, sent_hop, 0)
@@ -347,7 +375,7 @@
             final, final, out_send.at[0], out_recv.at[0], device_id=(d, last), device_id_type=MESH
         ).wait_recv()
 
-    values = final[0:1, :]
+    values = final[...]
     share = replicas // sections
     for j in range(share):
         out[j] = jnp.sum(jnp.where(iota(values.shape, 1) == s * share + j, values, 0.0))
@@ -390,21 +418,22 @@
             pltpu.VMEM((GROUPS * WINDOW, kv_width), BF16),
             pltpu.VMEM((chunks, CHUNK, GROUPS * WINDOW), F32),
             pltpu.VMEM((kv_width, GROUPS * WINDOW), BF16),
-            pltpu.VMEM((GROUPS * WINDOW, GROUPS * WINDOW), BF16),
+            pltpu.VMEM((GROUPS * WINDOW, kv_width), BF16),
             pltpu.VMEM((1, width), F32),
             pltpu.VMEM((8, 128), F32),
             pltpu.VMEM((8, 128), F32),
-            pltpu.VMEM((16, 128), F32),
-            pltpu.VMEM((replicas, 16, 128), F32),
             pltpu.VMEM((8, 128), F32),
+            pltpu.VMEM((replicas, 8, 128), F32),
+            pltpu.VMEM((1, 128), F32),
             pltpu.SemaphoreType.DMA((chunks,)),
             pltpu.SemaphoreType.DMA((2, PIECES)),
-            pltpu.SemaphoreType.DMA((chunks,)),
-            pltpu.SemaphoreType.DMA((chunks,)),
-            pltpu.SemaphoreType.DMA((replicas,)),
-            pltpu.SemaphoreType.DMA((replicas,)),
+            pltpu.SemaphoreType.DMA((chunks, PARTS)),
+            pltpu.SemaphoreType.DMA((chunks, PARTS)),
+            pltpu.SemaphoreType.DMA((1,)),
+            pltpu.SemaphoreType.DMA((1,)),
             pltpu.SemaphoreType.DMA((sections,)),
             pltpu.SemaphoreType.DMA((1,)),
+            pltpu.SemaphoreType.REGULAR,
         ],
         compiler_params=pltpu.CompilerParams(
             collective_id=0, has_side_effects=True, vmem_limit_bytes=56 << 20

time: 138 us -> 130 us (0.942)
  Pallas kernels: 135 us -> 126 us
    pallas_call x1, Pallas kernels: 135 us -> 126 us  [body(): pl.pallas_call(functools.partial(kernel, sections, replicas), out_shape=j...]
where the time goes in v2:
time: 130 us; the launch traced here: 128 us
  Pallas kernels  126 us (97%)
    pallas_call x1, Pallas kernels, body(): pl.pallas_call(functools.partial(kernel, sections, replicas), out_shape=j...  126 us

profile of v2, /device:TPU:6, one launch (start us, length us, event | category | flops | bytes accessed | tf_op | source)
XLA Modules:
  0.0 127.7 jit_solution(13282136629079755202)
XLA Ops:
  0.0 126.5 %slates.1 = f32[4]{0:T(128)} custom-call(bf16[288,5120]{1,0:T(8,128)(2,1)} %prompts.1, s32[1,32]{1,0:T(1,128)} %dest.1, s32[1,32]{1,0:T(1,128)} %start.1, s32[1,32]{1,0:T(1,128)} %pack.1, s32[6,1,32]{2,1,0:T(1,128)} %bitcast.4, s32[6,1,32]{2,1,0:T(1,128)} %bitcast.5, f32[1,5120]{1,0:T(1,128)} %gain.1, bf16[1,128,128]{2,1,0:T(8,128)(2,1)} %query.1, ...), custom_call_target="tpu_custom_call" | custom-call | tf_op jit(solution)/shard_map/slates/pallas_call | solution.py:406
  126.5 1.2 copy.14

commit v3 on v2

--- a/solution.py
+++ b/solution.py
@@ -15,8 +15,6 @@
 CHUNK = 16
 TAIL = 16
 WINDOW = CHUNK + TAIL
-PIECES = 4
-SPILL = 1024.0
 PARTS = 4
 
 BF16 = jnp.bfloat16
@@ -55,12 +53,13 @@
     ones_q,
     ones_k,
     weigh,
-    start_row,
+    start_for,
+    chosen,
     target,
     windows,
+    leaving,
     gathered,
     final,
-    x_sem,
     w_sem,
     recv_sem,
     send_sem,
@@ -68,7 +67,6 @@
     score_recv,
     out_send,
     out_recv,
-    turn,
 ):
     d = lax.axis_index("dp")
     s = lax.axis_index("section")
@@ -80,16 +78,18 @@
     kv_width = GROUPS * HEAD
     above = lax.rem(s + 1, sections)
     below = lax.rem(s + sections - 1, sections)
-    twin = d + 1 - 2 * lax.rem(d, 2)
 
     def chunk_rows(c):
         return pl.ds(pl.multiple_of(c * CHUNK, 16), CHUNK)
 
-    def x_copy(c):
-        return pltpu.make_async_copy(prompts.at[chunk_rows(c)], x.at[chunk_rows(c)], x_sem.at[c])
-
     part = width // PARTS
     part_groups = GROUPS // PARTS
+
+    def x_copy(c, p):
+        cols = pl.ds(p * part, part)
+        return pltpu.make_async_copy(
+            prompts.at[chunk_rows(c), cols], x.at[chunk_rows(c), cols], recv_sem.at[c, p]
+        )
 
     def hop(c, p):
         block = x.at[chunk_rows(c), pl.ds(p * part, part)]
@@ -98,27 +98,27 @@
             device_id=(d, above), device_id_type=MESH,
         )
 
-    piece = width // PIECES
-
-    def w_copies():
-        copies = []
-        for p in range(PIECES):
-            part = pl.ds(p * piece, piece)
-            copies.append(pltpu.make_async_copy(key_map.at[0, part], kw.at[part], w_sem.at[0, p]))
-            copies.append(pltpu.make_async_copy(value_map.at[0, part], vw.at[part], w_sem.at[1, p]))
-        return copies
+    def w_copies(p):
+        rows = pl.ds(p * part, part)
+        return [
+            pltpu.make_async_copy(key_map.at[0, rows], kw.at[rows], w_sem.at[0, p]),
+            pltpu.make_async_copy(value_map.at[0, rows], vw.at[rows], w_sem.at[1, p]),
+        ]
 
     @pl.when(s == 0)
     def _():
-        x_copy(0).start()
-
-    for copy in w_copies():
-        copy.start()
+        for p in range(PARTS):
+            x_copy(0, p).start()
+
+    for p in range(PARTS):
+        for copy in w_copies(p):
+            copy.start()
 
     @pl.when(s == 0)
     def _():
         def fetch(c, carry):
-            x_copy(c).start()
+            for p in range(PARTS):
+                x_copy(c, p).start()
             return carry
 
         lax.fori_loop(1, chunks, fetch, 0)
@@ -130,10 +130,6 @@
     @pl.when(s < last)
     def _():
         pl.semaphore_signal(barrier, inc=1, device_id=(d, last), device_id_type=MESH)
-
-    @pl.when(s == 0)
-    def _():
-        pl.semaphore_signal(barrier, inc=1, device_id=(twin, s), device_id_type=MESH)
 
     @pl.when(s == last)
     def _():
@@ -175,35 +171,32 @@
     @pl.when(s == last)
     def _():
         weigh[...] = final_gain[...] * score_vector[...].astype(F32).reshape(1, width)
-        column = jnp.sum(
+        diagonal = iota(square, 0) == iota(square, 1)
+
+        def as_column(row):
+            return jnp.sum(jnp.where(diagonal, row, 0.0), axis=1, keepdims=True)
+
+        start_for[:, 0:1] = jnp.sum(
             jnp.where(dest[...] == iota(square, 0), starts, 0.0), axis=1, keepdims=True
         )
-        start_row[0:1, 0:replicas] = jnp.sum(
-            jnp.where(iota(square, 0) == iota(square, 1), column, 0.0), axis=0, keepdims=True
-        )
         away = pack[...] - d
-        slot = jnp.where(away < 0, away + replicas, away).astype(F32) * 8.0
+        slot = jnp.where(away < 0, away + replicas, away).astype(F32)
+        chosen[:, 0:replicas] = jnp.where(iota(square, 1).astype(F32) == as_column(slot), 1.0, 0.0)
         for k in range(ITEMS):
             spot = jnp.zeros((1, replicas), F32)
             for i in range(ITEMS):
                 spot = spot + jnp.where(order[k] == i, items[i].astype(F32), 0.0)
-            target[k : k + 1, 0:replicas] = jnp.where(spot < 8.0, slot + spot, slot + SPILL)
+            target[:, k : k + 1] = as_column(spot)
         windows[...] = jnp.zeros_like(windows)
 
-    @pl.when(s == 0)
-    def _():
-        pl.semaphore_wait(barrier, 4)
-
-    @pl.when((s > 0) & (s < last))
-    def _():
-        pl.semaphore_wait(barrier, 3)
-
-    @pl.when(s == last)
-    def _():
-        pl.semaphore_wait(barrier, last + replicas + 1)
-
-    for copy in w_copies():
-        copy.wait()
+    def meet():
+        @pl.when(s < last)
+        def _():
+            pl.semaphore_wait(barrier, 3)
+
+        @pl.when(s == last)
+        def _():
+            pl.semaphore_wait(barrier, last + replicas + 1)
 
     def scale_of(states):
         return lax.rsqrt(jnp.mean(states * states, axis=1, keepdims=True) + EPS)
@@ -228,10 +221,7 @@
         values = jnp.zeros((CHUNK, kv_width), F32)
         queries, squares = [], []
         for p in range(PARTS):
-            @pl.when(s > 0)
-            def _():
-                hop(c, p).wait_recv()
-
+            hop(c, p).wait_recv()
             cols = slice(p * part, (p + 1) * part)
             states = x[rows, cols].astype(F32)
             energy = energy + jnp.sum(states * states, axis=1, keepdims=True)
@@ -278,36 +268,31 @@
             ]
             x[rows, cols] = (x[rows, cols].astype(F32) + jnp.concatenate(placed, axis=1)).astype(BF16)
 
-            if p == 0:
-                @pl.when((s == 0) & (c == 0) & (lax.rem(d, 2) == 1))
-                def _():
-                    pl.semaphore_wait(turn, 1)
-
-            @pl.when(s < last)
-            def _():
+        @pl.when(c == 0)
+        def _():
+            meet()
+
+        @pl.when(s < last)
+        def _():
+            for p in range(PARTS):
                 hop(c, p).start()
 
     def finish(c):
         states = x[chunk_rows(c), :].astype(F32)
         value = jnp.sum(states * weigh[...], axis=1, keepdims=True) * scale_of(states)
-        row = (iota((CHUNK, replicas), 0) + c * CHUNK).astype(F32)
-        offset = row - start_row[0:1, 0:replicas]
-        found = [
-            jnp.sum(jnp.where(offset == float(i), value, 0.0), axis=0, keepdims=True) for i in range(LMAX)
-        ]
-        windows[:, 0:replicas] += jnp.concatenate(found[0:8], axis=0)
-        windows[0:1, replicas : 2 * replicas] += found[8]
+        near = iota((CHUNK, CHUNK), 0) == iota((CHUNK, CHUNK), 1)
+        scores = jnp.sum(jnp.where(near, value, 0.0), axis=0, keepdims=True)
+        row = (iota((replicas, CHUNK), 1) + c * CHUNK).astype(F32)
+        offset = row - start_for[:, 0:1]
+        lane = iota(windows.shape, 1)
+        fresh = jnp.zeros(windows.shape, F32)
+        for i in range(LMAX):
+            found = jnp.sum(jnp.where(offset == float(i), scores, 0.0), axis=1, keepdims=True)
+            fresh = jnp.where(lane == i, found, fresh)
+        windows[...] += fresh
 
     def advance(c, carry):
-        @pl.when(s == 0)
-        def _():
-            x_copy(c).wait()
-
         block(c)
-
-        @pl.when((s == 0) & (c == 0) & (lax.rem(d, 2) == 0))
-        def _():
-            pl.semaphore_signal(turn, inc=1, device_id=(twin, s), device_id_type=MESH)
 
         @pl.when(s == last)
         def _():
@@ -315,6 +300,10 @@
 
         return carry
 
+    for p in range(PARTS):
+        for copy in w_copies(p):
+            copy.wait()
+
     lax.fori_loop(0, chunks, advance, 0)
 
     @pl.when(s == last)
@@ -322,32 +311,33 @@
         def score_copy(i):
             peer = lax.rem(d + replicas - i, replicas)
             return pltpu.make_async_remote_copy(
-                windows, gathered.at[i], score_send.at[0], score_recv.at[0],
+                leaving.at[peer], gathered.at[i], score_send.at[0], score_recv.at[0],
                 device_id=(peer, last), device_id_type=MESH,
             )
 
+        leaving[:, 0, :] = windows[...]
         others = gathered.at[pl.ds(1, replicas - 1)]
         for i in range(1, replicas):
             score_copy(i).start()
-        gathered[0] = windows[...]
+        gathered[0] = leaving[d]
         pltpu.make_async_copy(others, others, score_recv.at[0]).wait()
-        held = gathered[...]
-        lane = iota(gathered.shape, 2)
-        near = jnp.sum(jnp.where(lane == d, held, 0.0), axis=2, keepdims=True).reshape(replicas * 8, 1)
-        far = jnp.sum(jnp.where(lane == d + replicas, held, 0.0), axis=2, keepdims=True)
-        far = far.reshape(replicas * 8, 1)
-        place = iota((replicas * 8, replicas), 0).astype(F32)
-        ordered = []
-        for k in range(ITEMS):
-            wanted = target[k : k + 1, 0:replicas]
-            picked = jnp.where(place == wanted, near, 0.0) + jnp.where(place + SPILL == wanted, far, 0.0)
-            ordered.append(jnp.sum(picked, axis=0, keepdims=True))
-        tail = jnp.zeros((1, replicas), F32)
-        total = jnp.zeros((1, replicas), F32)
+        held = gathered[:, 0, :]
+        taken = jnp.zeros(held.shape, F32)
+        for i in range(replicas):
+            taken = taken + chosen[:, i : i + 1] * held[i : i + 1, :]
+        lane = iota(held.shape, 1).astype(F32)
+        ordered = [
+            jnp.sum(jnp.where(lane == target[:, k : k + 1], taken, 0.0), axis=1, keepdims=True)
+            for k in range(ITEMS)
+        ]
+        tail = jnp.zeros((replicas, 1), F32)
+        total = jnp.zeros((replicas, 1), F32)
         for k in reversed(range(ITEMS)):
             tail = tail + jnp.exp(ordered[k])
             total = total + (ordered[k] - jnp.log(tail))
-        final[0:1, 0:replicas] = total
+        final[0:1, 0:replicas] = jnp.sum(
+            jnp.where(iota(square, 0) == iota(square, 1), total, 0.0), axis=0, keepdims=True
+        )
 
         def out_copy(i):
             return pltpu.make_async_remote_copy(
@@ -420,20 +410,20 @@
             pltpu.VMEM((kv_width, GROUPS * WINDOW), BF16),
             pltpu.VMEM((GROUPS * WINDOW, kv_width), BF16),
             pltpu.VMEM((1, width), F32),
-            pltpu.VMEM((8, 128), F32),
-            pltpu.VMEM((8, 128), F32),
-            pltpu.VMEM((8, 128), F32),
-            pltpu.VMEM((replicas, 8, 128), F32),
+            pltpu.VMEM((replicas, 128), F32),
+            pltpu.VMEM((replicas, 128), F32),
+            pltpu.VMEM((replicas, 128), F32),
+            pltpu.VMEM((replicas, 128), F32),
+            pltpu.VMEM((replicas, 1, 128), F32),
+            pltpu.VMEM((replicas, 1, 128), F32),
             pltpu.VMEM((1, 128), F32),
-            pltpu.SemaphoreType.DMA((chunks,)),
-            pltpu.SemaphoreType.DMA((2, PIECES)),
+            pltpu.SemaphoreType.DMA((2, PARTS)),
             pltpu.SemaphoreType.DMA((chunks, PARTS)),
             pltpu.SemaphoreType.DMA((chunks, PARTS)),
             pltpu.SemaphoreType.DMA((1,)),
             pltpu.SemaphoreType.DMA((1,)),
             pltpu.SemaphoreType.DMA((sections,)),
             pltpu.SemaphoreType.DMA((1,)),
-            pltpu.SemaphoreType.REGULAR,
         ],
         compiler_params=pltpu.CompilerParams(
             collective_id=0, has_side_effects=True, vmem_limit_bytes=56 << 20

time: 130 us -> 127 us (0.977)
  Pallas kernels: 126 us -> 124 us
    pallas_call x1, Pallas kernels: 126 us -> 124 us  [body(): pl.pallas_call(functools.partial(kernel, sections, replicas), out_shape=j...]
where the time goes in v3:
time: 127 us; the launch traced here: 125 us
  Pallas kernels  124 us (98%)
    pallas_call x1, Pallas kernels, body(): pl.pallas_call(functools.partial(kernel, sections, replicas), out_shape=j...  124 us

profile of v3, /device:TPU:6, one launch (start us, length us, event | category | flops | bytes accessed | tf_op | source)
XLA Modules:
  0.0 125.2 jit_solution(962688673645662894)
XLA Ops:
  0.0 124.0 %slates.1 = f32[4]{0:T(128)} custom-call(bf16[288,5120]{1,0:T(8,128)(2,1)} %prompts.1, s32[1,32]{1,0:T(1,128)} %dest.1, s32[1,32]{1,0:T(1,128)} %start.1, s32[1,32]{1,0:T(1,128)} %pack.1, s32[6,1,32]{2,1,0:T(1,128)} %bitcast.4, s32[6,1,32]{2,1,0:T(1,128)} %bitcast.5, f32[1,5120]{1,0:T(1,128)} %gain.1, bf16[1,128,128]{2,1,0:T(8,128)(2,1)} %query.1, ...), custom_call_target="tpu_custom_call" | custom-call | tf_op jit(solution)/shard_map/slates/pallas_call | solution.py:396
  124.0 1.2 copy.14

commit v4 on v3

--- a/solution.py
+++ b/solution.py
@@ -30,6 +30,18 @@
     sections,
     replicas,
     prompts,
+    dest_in,
+    start_in,
+    pack_in,
+    items_in,
+    order_in,
+    gain_in,
+    query_in,
+    key_map,
+    value_map,
+    final_gain_in,
+    score_vector_in,
+    out,
     dest,
     start,
     pack,
@@ -37,11 +49,9 @@
     order,
     gain,
     query,
-    key_map,
-    value_map,
     final_gain,
     score_vector,
-    out,
+    in_sem,
     x,
     kw,
     vw,
@@ -83,7 +93,7 @@
         return pl.ds(pl.multiple_of(c * CHUNK, 16), CHUNK)
 
     part = width // PARTS
-    part_groups = GROUPS // PARTS
+    part_pairs = heads // 2 // PARTS
 
     def x_copy(c, p):
         cols = pl.ds(p * part, part)
@@ -110,9 +120,29 @@
         for p in range(PARTS):
             x_copy(0, p).start()
 
+    small = [
+        pltpu.make_async_copy(source, held, in_sem.at[i])
+        for i, (source, held) in enumerate(
+            (
+                (gain_in, gain),
+                (query_in, query),
+                (start_in, start),
+                (dest_in, dest),
+                (pack_in, pack),
+                (items_in, items),
+                (order_in, order),
+                (final_gain_in, final_gain),
+                (score_vector_in, score_vector),
+            )
+        )
+    ]
+    for copy in small[:3]:
+        copy.start()
     for p in range(PARTS):
         for copy in w_copies(p):
             copy.start()
+    for copy in small[3:]:
+        copy.start()
 
     @pl.when(s == 0)
     def _():
@@ -124,8 +154,9 @@
         lax.fori_loop(1, chunks, fetch, 0)
 
     barrier = pltpu.get_barrier_semaphore()
-    pl.semaphore_signal(barrier, inc=1, device_id=(d, above), device_id_type=MESH)
-    pl.semaphore_signal(barrier, inc=1, device_id=(d, below), device_id_type=MESH)
+    @pl.when(s > 0)
+    def _():
+        pl.semaphore_signal(barrier, inc=1, device_id=(d, below), device_id_type=MESH)
 
     @pl.when(s < last)
     def _():
@@ -133,18 +164,15 @@
 
     @pl.when(s == last)
     def _():
-        def greet_section(i, carry):
-            pl.semaphore_signal(barrier, inc=1, device_id=(d, i), device_id_type=MESH)
-            return carry
-
         def greet_replica(i, carry):
             peer = lax.rem(d + i, replicas)
             pl.semaphore_signal(barrier, inc=1, device_id=(peer, last), device_id_type=MESH)
             return carry
 
-        lax.fori_loop(0, last, greet_section, 0)
         lax.fori_loop(1, replicas, greet_replica, 0)
 
+    for copy in small[:3]:
+        copy.wait()
     pair[...] = jnp.zeros_like(pair)
     pair[0:HEAD, 0:HEAD] = query[0]
     pair[HEAD : 2 * HEAD, HEAD : 2 * HEAD] = query[0]
@@ -170,6 +198,8 @@
 
     @pl.when(s == last)
     def _():
+        for copy in small[3:]:
+            copy.wait()
         weigh[...] = final_gain[...] * score_vector[...].astype(F32).reshape(1, width)
         diagonal = iota(square, 0) == iota(square, 1)
 
@@ -192,20 +222,20 @@
     def meet():
         @pl.when(s < last)
         def _():
-            pl.semaphore_wait(barrier, 3)
+            pl.semaphore_wait(barrier, 1)
 
         @pl.when(s == last)
         def _():
-            pl.semaphore_wait(barrier, last + replicas + 1)
+            pl.semaphore_wait(barrier, last + replicas - 1)
 
     def scale_of(states):
         return lax.rsqrt(jnp.mean(states * states, axis=1, keepdims=True) + EPS)
 
     def by_group(parts):
         def head(b, j):
-            a = (b % part_groups) * per_group + j
-            p, half = divmod(a, 2)
-            values = parts[b // part_groups]
+            pair_of, half = divmod(b * per_group + j, 2)
+            home, p = divmod(pair_of, part_pairs)
+            values = parts[home]
             return values[p * CHUNK : (p + 1) * CHUNK, half * HEAD : (half + 1) * HEAD]
 
         return jnp.concatenate(
@@ -221,6 +251,11 @@
         values = jnp.zeros((CHUNK, kv_width), F32)
         queries, squares = [], []
         for p in range(PARTS):
+            @pl.when(c == 0)
+            def _():
+                for copy in w_copies(p):
+                    copy.wait()
+
             hop(c, p).wait_recv()
             cols = slice(p * part, (p + 1) * part)
             states = x[rows, cols].astype(F32)
@@ -255,18 +290,14 @@
             by_group(queries), kblock[...], (((1,), (1,)), ((), ())), preferred_element_type=F32
         )
         powers = jnp.exp(raw * factor + jnp.concatenate([bias[c]] * per_group, axis=0)).astype(BF16)
-        for p in range(PARTS):
-            near = slice(p * part_groups * HEAD, (p + 1) * part_groups * HEAD)
-            cols = slice(p * part, (p + 1) * part)
-            mixed = jnp.dot(powers, vblock[:, near], preferred_element_type=F32)
-            total = jnp.dot(powers, ones_k[:, near], preferred_element_type=F32)
-            mixed = mixed / total
-            placed = [
-                mixed[j * CHUNK : (j + 1) * CHUNK, b * HEAD : (b + 1) * HEAD]
-                for b in range(part_groups)
-                for j in range(per_group)
-            ]
-            x[rows, cols] = (x[rows, cols].astype(F32) + jnp.concatenate(placed, axis=1)).astype(BF16)
+        mixed = jnp.dot(powers, vblock[...], preferred_element_type=F32)
+        mixed = mixed / jnp.dot(powers, ones_k[...], preferred_element_type=F32)
+        placed = [
+            mixed[j * CHUNK : (j + 1) * CHUNK, b * HEAD : (b + 1) * HEAD]
+            for b in range(GROUPS)
+            for j in range(per_group)
+        ]
+        x[rows, :] = (x[rows, :].astype(F32) + jnp.concatenate(placed, axis=1)).astype(BF16)
 
         @pl.when(c == 0)
         def _():
@@ -299,10 +330,6 @@
             finish(c)
 
         return carry
-
-    for p in range(PARTS):
-        for copy in w_copies(p):
-            copy.wait()
 
     lax.fori_loop(0, chunks, advance, 0)
 
@@ -352,6 +379,9 @@
 
     @pl.when(s < last)
     def _():
+        for copy in small[3:]:
+            copy.wait()
+
         def sent_hop(c, carry):
             for p in range(PARTS):
                 hop(c, p).wait_send()
@@ -391,14 +421,23 @@
     rows, width = prompts.shape
     chunks = rows // CHUNK
     kv_width = GROUPS * HEAD
-    whole = pl.BlockSpec(memory_space=pltpu.VMEM)
     held = pl.BlockSpec(memory_space=pl.ANY)
     return pl.pallas_call(
         functools.partial(kernel, sections, replicas),
         out_shape=jax.ShapeDtypeStruct((replicas // sections,), F32),
-        in_specs=[held] + [whole] * 7 + [held, held] + [whole] * 2,
+        in_specs=[held] * 12,
         out_specs=pl.BlockSpec(memory_space=pltpu.SMEM),
         scratch_shapes=[
+            pltpu.VMEM((1, replicas), jnp.int32),
+            pltpu.VMEM((1, replicas), jnp.int32),
+            pltpu.VMEM((1, replicas), jnp.int32),
+            pltpu.VMEM((ITEMS, 1, replicas), jnp.int32),
+            pltpu.VMEM((ITEMS, 1, replicas), jnp.int32),
+            pltpu.VMEM((1, width), F32),
+            pltpu.VMEM((1, HEAD, HEAD), BF16),
+            pltpu.VMEM((1, width), F32),
+            pltpu.VMEM((width,), BF16),
+            pltpu.SemaphoreType.DMA((9,)),
             pltpu.VMEM((rows, width), BF16),
             pltpu.VMEM((width, kv_width), BF16),
             pltpu.VMEM((width, kv_width), BF16),

time: 127 us -> 124 us (0.976)
  Pallas kernels: 124 us -> 121 us
    pallas_call x1, Pallas kernels: 124 us -> 121 us  [body(): pl.pallas_call(functools.partial(kernel, sections, replicas), out_shape=j...]
where the time goes in v4:
time: 124 us; the launch traced here: 123 us
  Pallas kernels  121 us (98%)
    pallas_call x1, Pallas kernels, body(): pl.pallas_call(functools.partial(kernel, sections, replicas), out_shape=j...  121 us

profile of v4, /device:TPU:6, one launch (start us, length us, event | category | flops | bytes accessed | tf_op | source)
XLA Modules:
  0.0 122.7 jit_solution(2638050565879714157)
XLA Ops:
  0.0 121.5 %slates.1 = f32[4]{0:T(128)} custom-call(bf16[288,5120]{1,0:T(8,128)(2,1)} %prompts.1, s32[1,32]{1,0:T(1,128)} %dest_in.1, s32[1,32]{1,0:T(1,128)} %start_in.1, s32[1,32]{1,0:T(1,128)} %pack_in.1, s32[6,1,32]{2,1,0:T(1,128)} %bitcast.4, s32[6,1,32]{2,1,0:T(1,128)} %bitcast.5, f32[1,5120]{1,0:T(1,128)} %gain_in.1, bf16[1,128,128]{2,1,0:T(8,128)(2,1)} %query_in.1, ...), custom_call_target="tpu_custom_call" | custom-call | tf_op jit(solution)/shard_map/slates/pallas_call | solution.py:425
  121.5 1.2 copy.14

commit v5 on v4

--- a/solution.py
+++ b/solution.py
@@ -15,7 +15,7 @@
 CHUNK = 16
 TAIL = 16
 WINDOW = CHUNK + TAIL
-PARTS = 4
+PARTS = 5
 
 BF16 = jnp.bfloat16
 F32 = jnp.float32
@@ -196,6 +196,12 @@
 
     square = (replicas, replicas)
 
+    def steps_to(other):
+        y = lax.rem(other // 8 - d // 8 + 4, 4)
+        across = lax.rem(lax.rem(other // 2, 4) - lax.rem(d // 2, 4) + 4, 4)
+        core = lax.rem(lax.rem(other, 2) - lax.rem(d, 2) + 2, 2)
+        return y * 8 + across * 2 + core
+
     @pl.when(s == last)
     def _():
         for copy in small[3:]:
@@ -209,8 +215,7 @@
         start_for[:, 0:1] = jnp.sum(
             jnp.where(dest[...] == iota(square, 0), starts, 0.0), axis=1, keepdims=True
         )
-        away = pack[...] - d
-        slot = jnp.where(away < 0, away + replicas, away).astype(F32)
+        slot = steps_to(pack[...]).astype(F32)
         chosen[:, 0:replicas] = jnp.where(iota(square, 1).astype(F32) == as_column(slot), 1.0, 0.0)
         for k in range(ITEMS):
             spot = jnp.zeros((1, replicas), F32)
@@ -336,7 +341,10 @@
     @pl.when(s == last)
     def _():
         def score_copy(i):
-            peer = lax.rem(d + replicas - i, replicas)
+            y = lax.rem(d // 8 + 4 - i // 8, 4)
+            across = lax.rem(lax.rem(d // 2, 4) + 4 - i // 2 % 4, 4)
+            core = lax.rem(lax.rem(d, 2) + i, 2)
+            peer = y * 8 + across * 2 + core
             return pltpu.make_async_remote_copy(
                 leaving.at[peer], gathered.at[i], score_send.at[0], score_recv.at[0],
                 device_id=(peer, last), device_id_type=MESH,
@@ -344,7 +352,10 @@
 
         leaving[:, 0, :] = windows[...]
         others = gathered.at[pl.ds(1, replicas - 1)]
-        for i in range(1, replicas):
+        def links(i):
+            return min(i // 8, 4 - i // 8) + min(i // 2 % 4, 4 - i // 2 % 4)
+
+        for i in sorted(range(1, replicas), key=lambda i: -links(i)):
             score_copy(i).start()
         gathered[0] = leaving[d]
         pltpu.make_async_copy(others, others, score_recv.at[0]).wait()

time: 124 us -> 124 us (level)
  no operation moved by 1% of the time
where the time goes in v5:
time: 124 us; the launch traced here: 122 us
  Pallas kernels  121 us (98%)
    pallas_call x1, Pallas kernels, body(): pl.pallas_call(functools.partial(kernel, sections, replicas), out_shape=j...  121 us

profile of v5, /device:TPU:6, one launch (start us, length us, event | category | flops | bytes accessed | tf_op | source)
XLA Modules:
  0.0 122.4 jit_solution(18265863314089585329)
XLA Ops:
  0.0 121.2 %slates.1 = f32[4]{0:T(128)} custom-call(bf16[288,5120]{1,0:T(8,128)(2,1)} %prompts.1, s32[1,32]{1,0:T(1,128)} %dest_in.1, s32[1,32]{1,0:T(1,128)} %start_in.1, s32[1,32]{1,0:T(1,128)} %pack_in.1, s32[6,1,32]{2,1,0:T(1,128)} %bitcast.4, s32[6,1,32]{2,1,0:T(1,128)} %bitcast.5, f32[1,5120]{1,0:T(1,128)} %gain_in.1, bf16[1,128,128]{2,1,0:T(8,128)(2,1)} %query_in.1, ...), custom_call_target="tpu_custom_call" | custom-call | tf_op jit(solution)/shard_map/slates/pallas_call | solution.py:436
  121.2 1.2 copy.14

commit v6 on v4

--- a/solution.py
+++ b/solution.py
@@ -243,7 +243,7 @@
             axis=0,
         )
 
-    def block(c):
+    def block(c, opening):
         rows = chunk_rows(c)
         old = kv[...]
         energy = jnp.zeros((CHUNK, 1), F32)
@@ -251,8 +251,7 @@
         values = jnp.zeros((CHUNK, kv_width), F32)
         queries, squares = [], []
         for p in range(PARTS):
-            @pl.when(c == 0)
-            def _():
+            if opening:
                 for copy in w_copies(p):
                     copy.wait()
 
@@ -299,8 +298,7 @@
         ]
         x[rows, :] = (x[rows, :].astype(F32) + jnp.concatenate(placed, axis=1)).astype(BF16)
 
-        @pl.when(c == 0)
-        def _():
+        if opening:
             meet()
 
         @pl.when(s < last)
@@ -323,7 +321,7 @@
         windows[...] += fresh
 
     def advance(c, carry):
-        block(c)
+        block(c, False)
 
         @pl.when(s == last)
         def _():
@@ -331,7 +329,13 @@
 
         return carry
 
-    lax.fori_loop(0, chunks, advance, 0)
+    block(0, True)
+
+    @pl.when(s == last)
+    def _():
+        finish(0)
+
+    lax.fori_loop(1, chunks, advance, 0)
 
     @pl.when(s == last)
     def _():

time: 124 us -> 124 us (level)
  no operation moved by 1% of the time
where the time goes in v6:
time: 124 us; the launch traced here: 123 us
  Pallas kernels  121 us (98%)
    pallas_call x1, Pallas kernels, body(): pl.pallas_call(functools.partial(kernel, sections, replicas), out_shape=j...  121 us

profile of v6, /device:TPU:6, one launch (start us, length us, event | category | flops | bytes accessed | tf_op | source)
XLA Modules:
  0.0 122.7 jit_solution(5977746552603492845)
XLA Ops:
  0.0 121.5 %slates.1 = f32[4]{0:T(128)} custom-call(bf16[288,5120]{1,0:T(8,128)(2,1)} %prompts.1, s32[1,32]{1,0:T(1,128)} %dest_in.1, s32[1,32]{1,0:T(1,128)} %start_in.1, s32[1,32]{1,0:T(1,128)} %pack_in.1, s32[6,1,32]{2,1,0:T(1,128)} %bitcast.4, s32[6,1,32]{2,1,0:T(1,128)} %bitcast.5, f32[1,5120]{1,0:T(1,128)} %gain_in.1, bf16[1,128,128]{2,1,0:T(8,128)(2,1)} %query_in.1, ...), custom_call_target="tpu_custom_call" | custom-call | tf_op jit(solution)/shard_map/slates/pallas_call | solution.py:429
  121.5 1.2 copy.14
